TPU v7x, 32 devices: a whole 2x2x4 slice. The times are simulated.
32 devices in a mesh: diag: 4 (over z), long: 8 (over y, x, core).
Axes of the slice: x: 2, y: 2, z: 4, core: 2. Of those that a mesh axis runs over, the one named last changes fastest.
Arguments:
- tiles: bfloat16 [4, 8, 512, 128, 128], P('diag', 'long'), may hold values from -0.0546875 to 0.0546875
- tile_rows: int32 [4, 8, 512], P('diag', 'long'), may hold values from 0 to 23, as said below
- tile_cols: int32 [4, 8, 512], P('diag', 'long'), may hold values from 0 to 47, as said below
- tile_counts: int32 [4, 8], P('diag', 'long'), may hold values from 0 to 512, as said below
- block_x: bfloat16 [16, 24576], P(None, 'long'), may hold values from -16 to 16
- block_p: bfloat16 [16, 24576], P(None, 'long'), may hold values from -16 to 16
Outputs:
- ritz_basis: float32 [48, 24576], P(None, 'long')
- ritz_image: float32 [48, 24576], P(None, 'long')
- ritz_matrix: float32 [48, 48], replicated
Inputs may be any that keep to these rules, and one draw needn't show every extreme that they name: `tile_rows`: each entry is a tile row of the row panel of its grid position. `tile_cols`: each entry is a tile column of the two panels of the segment of its grid position; for live entries the global tile column never exceeds the global tile row, and no pair of tile row and column repeats within one list. `tile_counts`: entries of a list past its count are ignored. A count never exceeds the pairs of its grid position on or below the diagonal; the last grid column of grid row 0 is full.
All inputs are finite; a program needn't handle non-finite values.
Results may differ from a plain program's by a relative error of at most 0.0004.
The roundings to bfloat16 on the way count: a program that leaves them out, or rounds other values in their place, can miss the bound.
Values may be sent and summed in bfloat16 or wider, within the bound.
A program may use at most 128 MiB of HBM per device.

v0:
```python
import jax
import jax.numpy as jnp
from jax import lax
from jax.sharding import PartitionSpec as P


def local(tiles, tile_rows, tile_cols, tile_counts, block_x, block_p):
    highest = lax.Precision.HIGHEST
    tile_block = tiles[0, 0]
    rows = tile_rows[0, 0]
    cols = tile_cols[0, 0]
    count = tile_counts[0, 0]
    slot_count = tile_block.shape[0]
    edge = tile_block.shape[-1]
    panel_rows = block_x.shape[1]
    panel_tiles = panel_rows // edge
    diag_index = lax.axis_index("diag")
    long_index = lax.axis_index("long")
    long_size = lax.axis_size("long")
    diag_size = lax.axis_size("diag")
    folded = long_index < 2 * diag_index
    row_panel = jnp.where(folded, long_size - 1 - long_index, long_index)
    segment_id = jnp.where(folded, diag_size - 1 - diag_index, diag_index)
    valid = (jnp.arange(slot_count, dtype=jnp.int32) < count).astype(jnp.float32)
    same = row_panel * panel_tiles + rows == 2 * segment_id * panel_tiles + cols
    weight = jnp.where(same, 0.5, 1.0).astype(jnp.float32) * valid

    def apply_hamiltonian(vectors):
        count_vec = vectors.shape[0]
        whole = lax.all_gather(vectors, "long", axis=1, tiled=True)
        segment = lax.dynamic_slice_in_dim(whole, 2 * segment_id * panel_rows, 2 * panel_rows, 1)
        own = lax.dynamic_slice_in_dim(whole, row_panel * panel_rows, panel_rows, 1)
        segment_tiles = segment.reshape(count_vec, 2 * panel_tiles, edge)
        own_tiles = own.reshape(count_vec, panel_tiles, edge)
        forward = jnp.einsum(
            "kab,vkb->vka",
            tile_block,
            jnp.take(segment_tiles, cols, axis=1),
            preferred_element_type=jnp.float32,
        )
        row_part = (
            jnp.zeros((count_vec, panel_tiles, edge), jnp.float32)
            .at[:, rows, :]
            .add(forward * weight[None, :, None])
            .reshape(count_vec, panel_rows)
        )
        backward = jnp.einsum(
            "kab,vka->vkb",
            tile_block,
            jnp.take(own_tiles, rows, axis=1),
            preferred_element_type=jnp.float32,
        )
        col_part = (
            jnp.zeros((count_vec, 2 * panel_tiles, edge), jnp.float32)
            .at[:, cols, :]
            .add(backward * weight[None, :, None])
            .reshape(count_vec, 2 * panel_rows)
        )
        empty = jnp.zeros((count_vec, long_size * panel_rows), jnp.float32)
        spread = lax.dynamic_update_slice_in_dim(empty, col_part, 2 * segment_id * panel_rows, 1)
        spread = spread + lax.dynamic_update_slice_in_dim(
            empty, row_part, row_panel * panel_rows, 1
        )
        total = lax.psum_scatter(spread, "long", scatter_dimension=1, tiled=True)
        return lax.psum(total, "diag")

    width = block_x.shape[0]
    first = apply_hamiltonian(jnp.concatenate([block_x, block_p], 0))
    image_x = first[:width]
    image_p = first[width:]
    block_float = block_x.astype(jnp.float32)
    numerator, denominator = lax.psum(
        (jnp.sum(block_float * image_x, axis=1), jnp.sum(block_float * block_float, axis=1)), "long"
    )
    quotient = numerator / denominator
    search = (image_x - quotient[:, None] * block_float).astype(jnp.bfloat16)
    image_w = apply_hamiltonian(search)
    basis_in = jnp.concatenate([block_x, search, block_p], 0).astype(jnp.float32)
    himage = jnp.concatenate([image_x, image_w, image_p], 0)
    gram, projected = lax.psum(
        (
            jnp.dot(basis_in, basis_in.T, precision=highest),
            jnp.dot(basis_in, himage.T, precision=highest),
        ),
        "long",
    )
    factor = jnp.linalg.cholesky(gram)
    subspace = gram.shape[0]
    inverse = jax.scipy.linalg.solve_triangular(
        factor, jnp.eye(subspace, dtype=jnp.float32), lower=True
    )
    ritz_basis = jnp.dot(inverse, basis_in, precision=highest)
    ritz_image = jnp.dot(inverse, himage, precision=highest)
    reduced = jnp.dot(jnp.dot(inverse, projected, precision=highest), inverse.T, precision=highest)
    ritz_matrix = 0.5 * (reduced + reduced.T)
    return (ritz_basis, ritz_image, ritz_matrix)


def solution(mesh):
    return jax.shard_map(
        local,
        mesh=mesh,
        in_specs=(
            P("diag", "long", None, None, None),
            P("diag", "long", None),
            P("diag", "long", None),
            P("diag", "long"),
            P(None, "long"),
            P(None, "long"),
        ),
        out_specs=(P(None, "long"), P(None, "long"), P()),
        check_vma=False,
    )
```

profile of v0, /device:TPU:0, one launch (start us, length us, event | category | flops | bytes accessed | tf_op | source)
XLA Modules:
  0.0 512.1 jit_solution(18298407920136523371)
XLA Ops:
  7.2 1.6 pad_maximum_fusion.4
  9.6 0.7 compare_select_fusion
  10.3 0.7 compare_and_fusion
  11.0 0.7 select_select_fusion.1
  11.7 27.2 %all-gather.2.cloned.1.call-done = bf16[32,24576]{1,0:T(8,128)(2,1)} async-done(((bf16[32,3072]{1,0:T(8,128)(2,1)}), bf16[32,24576]{1,0:T(8,128)(2,1)}) %all-gather.2.cloned.1.call-update) | async-done | bytes 1572880 | tf_op jit(solution)/shard_map/all_gather | solution.py:30
  38.9 1.0 copy_bitcast_fusion.2
  39.9 3.5 gather_fusion
  43.3 12.0 %broadcast_multiply_fusion.1 = f32[512,32,128]{2,1,0:T(8,128)} fusion(f32[512]{0:T(512)S(1)} %select_select_fusion.1, bf16[1,1,512,128,128]{4,3,2,1,0:T(8,128)(2,1)} %param.6, bf16[512,32,128]{2,1,0:T(8,128)(2,1)} %gather_fusion, pred[512]{0:T(512)(128)(4,1)S(1)} %get-tuple-element.14), kind=kOutput, calls=%fused_computation.21 | convolution fusion | flops 541065216 | bytes 29362688 | tf_op jit(solution)/shard_map/kab,vka->vkb/dot_general | solution.py:47
  55.3 0.1 broadcast_in_dim.74
  55.4 44.7 %scatter_fusion = f32[32,48,128]{2,0,1:T(8,128)S(1)} fusion(f32[32,48,128]{2,0,1:T(8,128)S(1)} %broadcast_in_dim.74, s32[512]{0:T(512)S(1)} %bitcast.114, f32[512,32,128]{2,1,0:T(8,128)} %broadcast_multiply_fusion.1), kind=kCustom, calls=%fused_computation.4 | custom fusion | flops 2097152 | bytes 25167872 | tf_op jit(solution)/shard_map/scatter-add | solution.py:56
  100.1 0.2 broadcast_in_dim.73
  100.4 1.7 copy-done
  102.0 1.1 copy_bitcast_fusion
  103.1 3.5 gather_fusion.1
  106.6 16.2 %broadcast_multiply_fusion = f32[512,32,128]{2,1,0:T(8,128)} fusion(f32[512]{0:T(512)S(1)} %select_select_fusion.1, bf16[1,1,512,128,128]{4,3,2,1,0:T(8,128)(2,1)} %param.6, bf16[512,32,128]{2,1,0:T(8,128)(2,1)} %gather_fusion.1, pred[512]{0:T(512)(128)(4,1)S(1)} %get-tuple-element.13), kind=kOutput, calls=%fused_computation.20 | convolution fusion | flops 541065216 | bytes 29362688 | tf_op jit(solution)/shard_map/kab,vkb->vka/dot_general | solution.py:35
  122.9 45.1 %scatter_fusion.1 = f32[32,24,128]{2,0,1:T(8,128)S(1)} fusion(f32[32,24,128]{2,0,1:T(8,128)S(1)} %broadcast_in_dim.79, s32[512]{0:T(512)S(1)} %bitcast.111, f32[512,32,128]{2,1,0:T(8,128)} %broadcast_multiply_fusion), kind=kCustom, calls=%fused_computation.5 | custom fusion | flops 2097152 | bytes 25167872 | tf_op jit(solution)/shard_map/scatter-add | solution.py:44
  168.0 1.9 fusion.42
  169.9 46.3 %reduce-scatter.3.cloned.1.call-done = f32[32,3072]{1,0:T(8,128)} async-done(((f32[32,24576]{1,0:T(8,128)}), f32[32,3072]{1,0:T(8,128)}) %reduce-scatter.3.cloned.1.call-update) | async-done | bytes 393232 | tf_op jit(solution)/shard_map/reduce_scatter | solution.py:64
  216.2 39.5 %all-reduce.5.cloned.1.call-done = f32[32,3072]{1,0:T(8,128)} async-done(((f32[32,3072]{1,0:T(8,128)}), f32[32,3072]{1,0:T(8,128)}) %all-reduce.5.cloned.1.call-update) | async-done | bytes 393232 | tf_op jit(solution)/shard_map/psum | solution.py:65
  255.7 1.2 fusion.44
  256.9 11.9 %all-reduce.1 = (f32[16]{0:T(128)S(1)}, f32[16]{0:T(128)S(1)}) all-reduce(f32[16]{0:T(128)S(1)} %get-tuple-element.4, f32[16]{0:T(128)S(1)} %get-tuple-element.3), channel_id=1, replica_groups=mesh['diag'=4,'long'=8] {'long'}, use_global_device_ids=true, to_apply=%region_5.6 | all-reduce | flops 32 | bytes 256 | tf_op jit(solution)/shard_map/psum | solution.py:72
  268.8 1.0 fusion.46
  269.8 10.3 %all_gather.7 = bf16[16,24576]{1,0:T(8,128)(2,1)S(1)} all-gather(bf16[16,3072]{1,0:T(8,128)(2,1)S(1)} %fusion.46), channel_id=1, replica_groups=mesh['diag'=4,'long'=8] {'long'}, dimensions={1}, use_global_device_ids=true | all-gather | bytes 884736 | tf_op jit(solution)/shard_map/all_gather | solution.py:30
  280.2 2.0 gather_fusion.2
  282.2 10.7 %broadcast_multiply_fusion.3 = f32[512,16,128]{2,1,0:T(8,128)} fusion(f32[512]{0:T(512)S(1)} %select_select_fusion.1, bf16[1,1,512,128,128]{4,3,2,1,0:T(8,128)(2,1)} %param.6, bf16[512,16,128]{2,1,0:T(8,128)(2,1)S(1)} %gather_fusion.2, pred[512]{0:T(512)(128)(4,1)S(1)} %get-tuple-element.14), kind=kOutput, calls=%fused_computation.31 | convolution fusion | flops 270532608 | bytes 23071232 | tf_op jit(solution)/shard_map/kab,vka->vkb/dot_general | solution.py:47
  292.9 2.0 gather_fusion.3
  294.9 15.0 %broadcast_multiply_fusion.2 = f32[512,16,128]{2,1,0:T(8,128)} fusion(f32[512]{0:T(512)S(1)} %select_select_fusion.1, bf16[1,1,512,128,128]{4,3,2,1,0:T(8,128)(2,1)} %param.6, bf16[512,16,128]{2,1,0:T(8,128)(2,1)S(1)} %gather_fusion.3, pred[512]{0:T(512)(128)(4,1)S(1)} %get-tuple-element.13), kind=kOutput, calls=%fused_computation.30 | convolution fusion | flops 270532608 | bytes 23071232 | tf_op jit(solution)/shard_map/kab,vkb->vka/dot_general | solution.py:35
  309.9 40.3 %scatter_fusion.2 = f32[16,48,128]{2,0,1:T(8,128)S(1)} fusion(f32[16,48,128]{2,0,1:T(8,128)S(1)} %broadcast_in_dim.82, s32[512]{0:T(512)S(1)} %bitcast.115, f32[512,16,128]{2,1,0:T(8,128)} %broadcast_multiply_fusion.3), kind=kCustom, calls=%fused_computation.6 | custom fusion | flops 1048576 | bytes 12584960 | tf_op jit(solution)/shard_map/scatter-add | solution.py:56
  350.2 0.1 broadcast_in_dim.81
  350.4 40.9 %scatter_fusion.3 = f32[16,24,128]{2,0,1:T(8,128)S(1)} fusion(f32[16,24,128]{2,0,1:T(8,128)S(1)} %broadcast_in_dim.85, s32[512]{0:T(512)S(1)} %bitcast.112, f32[512,16,128]{2,1,0:T(8,128)} %broadcast_multiply_fusion.2), kind=kCustom, calls=%fused_computation.7 | custom fusion | flops 1048576 | bytes 12584960 | tf_op jit(solution)/shard_map/scatter-add | solution.py:44
  391.3 1.1 copy-done.1
  392.5 37.5 %reduce-scatter.5.cloned.1.call-done = f32[16,3072]{1,0:T(8,128)} async-done(((f32[16,24576]{1,0:T(8,128)}), f32[16,3072]{1,0:T(8,128)}) %reduce-scatter.5.cloned.1.call-update) | async-done | bytes 196624 | tf_op jit(solution)/shard_map/reduce_scatter | solution.py:64
  430.1 0.2 fusion.60
  430.3 36.7 %all-reduce.7.cloned.1.call-done = f32[16,3072]{1,0:T(8,128)} async-done(((f32[16,3072]{1,0:T(8,128)}), f32[16,3072]{1,0:T(8,128)}) %all-reduce.7.cloned.1.call-update) | async-done | bytes 196624 | tf_op jit(solution)/shard_map/psum | solution.py:65
  467.0 1.3 fusion.40
  468.4 23.0 %all-reduce = (f32[48,48]{0,1:T(8,128)S(1)}, f32[48,48]{1,0:T(8,128)S(1)}) all-reduce(f32[48,48]{0,1:T(8,128)S(1)} %fusion.60, f32[48,48]{1,0:T(8,128)S(1)} %fusion.40), channel_id=1, replica_groups=mesh['diag'=4,'long'=8] {'long'}, use_global_device_ids=true, to_apply=%region_8.9 | all-reduce | flops 4608 | bytes 36864 | tf_op jit(solution)/shard_map/psum | solution.py:80
  491.3 0.1 copy.24
  491.4 4.4 cholesky.17
  495.8 0.6 compare_reduce_fusion
  496.5 0.7 fusion.48
  497.1 3.7 custom-call.7
  500.8 0.2 fusion.50
  501.0 1.2 fusion.59
  502.2 0.1 fusion.61
  502.4 0.2 fusion.62
  502.6 0.1 copy.29
  502.6 0.6 fusion.49
  503.3 2.4 fusion.41
  (29 shorter events, 0.6 us)
Async XLA Ops:
  7.2 31.7 %all-gather.2.cloned.1.call-start = ((), (), s32[]{:S(2)}) async-start(), calls=%async_computation.2 | async-start | bytes 1769472 | tf_op jit(solution)/shard_map/all_gather | solution.py:30
  8.9 207.3 %reduce-scatter.3.cloned.1.call-start = ((), (), s32[]{:S(2)}) async-start(), calls=%async_computation.3 | async-start | bytes 3538944 | tf_op jit(solution)/shard_map/reduce_scatter | solution.py:64
  100.4 1.7 copy-start
  168.0 87.8 %copy-start.2 = (bf16[16,3072]{1,0:T(8,128)(2,1)S(1)}, bf16[16,3072]{1,0:T(8,128)(2,1)}, u32[]{:S(2)}) copy-start(bf16[16,3072]{1,0:T(8,128)(2,1)} %param.10) | copy-start | bytes 294916
  169.8 85.9 %all-reduce.5.cloned.1.call-start = ((), (), s32[]{:S(2)}) async-start(), calls=%async_computation.4 | async-start | bytes 786432 | tf_op jit(solution)/shard_map/psum | solution.py:65
  216.2 213.8 %reduce-scatter.5.cloned.1.call-start = ((), (), s32[]{:S(2)}) async-start(), calls=%async_computation.5 | async-start | bytes 1769472 | tf_op jit(solution)/shard_map/reduce_scatter | solution.py:64
  350.4 79.7 %copy-start.3 = (bf16[16,3072]{1,0:T(8,128)(2,1)S(1)}, bf16[16,3072]{1,0:T(8,128)(2,1)}, u32[]{:S(2)}) copy-start(bf16[16,3072]{1,0:T(8,128)(2,1)} %param.11) | copy-start | bytes 294916
  391.3 1.2 copy-start.1
  392.5 74.5 %all-reduce.7.cloned.1.call-start = ((), (), s32[]{:S(2)}) async-start(), calls=%async_computation.6 | async-start | bytes 393216 | tf_op jit(solution)/shard_map/psum | solution.py:65
Sparse Core Ops, SparseCore 0:
  10.5 28.3 all-gather.1
  170.0 46.1 reduce-scatter.2
  218.6 37.0 all-reduce.4
  392.6 37.3 reduce-scatter.4
  432.2 34.7 all-reduce.6
where the time goes:
time: 516 us; the launch traced here: 512 us
  other arithmetic  189 us (37%)
  waiting for transfers between devices  187 us (36%)
  matrix products  59.5 us (12%)
  blocking collectives  45.1 us (9%)
  local copies, waits for them, and re-layouts  16.6 us (3%)
  between operations  14.7 us (3%)
    scatter-add x2, other arithmetic, apply_hamiltonian(): row_part = jnp.zeros((count_vec, panel_tiles, edge), jnp.float32).at[:, r...  85.9 us
    scatter-add x2, other arithmetic, apply_hamiltonian(): col_part = jnp.zeros((count_vec, 2 * panel_tiles, edge), jnp.float32).at[...  85 us
    reduce_scatter x2, waiting for transfers between devices, apply_hamiltonian(): total = lax.psum_scatter(spread, 'long', scatter_dimension=1, tiled=True)  83.8 us
    psum x2, waiting for transfers between devices, apply_hamiltonian(): return lax.psum(total, 'diag')  76.2 us
    dot_general x2, matrix products, apply_hamiltonian(): jnp.einsum('kab,vkb->vka', tile_block, jnp.take(segment_tiles, cols, axis...  31.2 us
    all_gather x1, waiting for transfers between devices, apply_hamiltonian(): whole = lax.all_gather(vectors, 'long', axis=1, tiled=True)  27.2 us
    psum x1, blocking collectives, local(): lax.psum((jnp.dot(basis_in, basis_in.T, precision=highest), jnp.dot(basis...  23 us
    dot_general x2, matrix products, apply_hamiltonian(): jnp.einsum('kab,vka->vkb', tile_block, jnp.take(own_tiles, rows, axis=1),...  22.6 us
  transfers between devices with their start and end apart: 5, of which 5 were waited for; matrix products, arithmetic and copies ran while one was open for 0% of the time, Pallas kernels for 0%

commit v1 on v0

v1 whole, which is shorter than its diff:
```python
import functools

import jax
import jax.numpy as jnp
from jax import lax
from jax.experimental import pallas as pl
from jax.experimental.pallas import tpu as pltpu
from jax.sharding import PartitionSpec as P

HIGHEST = lax.Precision.HIGHEST
STEP = 64
UNROLL = 8


def tile_kernel(rows_ref, cols_ref, meta_ref, vec_ref, tile_ref, out_ref):
    edge = tile_ref.shape[-1]
    base = pl.program_id(0) * STEP

    @pl.when(pl.program_id(0) == 0)
    def _():
        out_ref[...] = jnp.zeros_like(out_ref)

    count, row_off, col_off = meta_ref[0], meta_ref[1], meta_ref[2]
    live = jnp.clip(count - base, 0, STEP)

    def group(i, carry):
        spots = []
        for u in range(UNROLL):
            k = i * UNROLL + u
            row = rows_ref[base + k] + row_off
            col = cols_ref[base + k] + col_off
            weight = jnp.where(row == col, 0.5, 1.0).astype(jnp.float32)
            weight = jnp.where(base + k < count, weight, 0.0)
            row_at = pl.ds(pl.multiple_of(row * edge, edge), edge)
            col_at = pl.ds(pl.multiple_of(col * edge, edge), edge)
            tile = tile_ref[k]
            forward = lax.dot_general(
                vec_ref[:, col_at],
                tile,
                (((1,), (1,)), ((), ())),
                preferred_element_type=jnp.float32,
            )
            backward = jnp.dot(vec_ref[:, row_at], tile, preferred_element_type=jnp.float32)
            spots.append((row_at, col_at, forward * weight, backward * weight))
        for row_at, col_at, forward, backward in spots:
            out_ref[:, row_at] += forward
            out_ref[:, col_at] += backward
        return carry

    lax.fori_loop(0, (live + UNROLL - 1) // UNROLL, group, 0)


def apply_tiles(tiles, rows, cols, meta, vectors):
    slots, edge = tiles.shape[0], tiles.shape[-1]
    width, states = vectors.shape
    smem = pl.BlockSpec(memory_space=pltpu.SMEM)
    return pl.pallas_call(
        tile_kernel,
        grid=(slots // STEP,),
        in_specs=[
            smem,
            smem,
            smem,
            pl.BlockSpec(memory_space=pltpu.VMEM),
            pl.BlockSpec((STEP, edge, edge), lambda i: (i, 0, 0)),
        ],
        out_specs=pl.BlockSpec((width, states), lambda i: (0, 0)),
        out_shape=jax.ShapeDtypeStruct((width, states), jnp.float32),
        compiler_params=pltpu.CompilerParams(vmem_limit_bytes=40 << 20),
        cost_estimate=pl.CostEstimate(
            flops=4 * slots * edge * edge * width,
            bytes_accessed=2 * slots * edge * edge,
            transcendentals=0,
        ),
    )(rows, cols, meta, vectors, tiles)


def ritz_kernel(gram_ref, proj_ref, basis_ref, image_ref, rb_ref, ri_ref, rm_ref):
    size = gram_ref.shape[0]
    lane = lax.broadcasted_iota(jnp.int32, (size, size), 1)
    row = lax.broadcasted_iota(jnp.int32, (size, size), 0)
    below = lax.broadcasted_iota(jnp.int32, (size, 1), 0)
    left = gram_ref[...]
    right = jnp.where(lane == row, 1.0, 0.0).astype(jnp.float32)
    pivots = jnp.zeros((size, 1), jnp.float32)
    for k in range(size):
        pivot = left[k : k + 1, k : k + 1]
        pivots = jnp.where(below == k, pivot, pivots)
        scale = jnp.where(below > k, left[:, k : k + 1] * (1.0 / pivot), 0.0)
        left_row, right_row = left[k : k + 1, :], right[k : k + 1, :]
        left = left - scale * left_row
        right = right - scale * right_row
    inverse = right * (1.0 / jnp.sqrt(pivots))
    nt = (((1,), (1,)), ((), ()))
    half = jnp.dot(inverse, proj_ref[...], precision=HIGHEST, preferred_element_type=jnp.float32)
    one = lax.dot_general(half, inverse, nt, precision=HIGHEST, preferred_element_type=jnp.float32)
    two = lax.dot_general(inverse, half, nt, precision=HIGHEST, preferred_element_type=jnp.float32)
    rm_ref[...] = 0.5 * (one + two)
    rb_ref[...] = jnp.dot(
        inverse, basis_ref[...].astype(jnp.float32), precision=HIGHEST, preferred_element_type=jnp.float32
    )
    ri_ref[...] = jnp.dot(
        inverse, image_ref[...], precision=HIGHEST, preferred_element_type=jnp.float32
    )


def ritz(gram, projected, basis, image):
    vmem = pl.BlockSpec(memory_space=pltpu.VMEM)
    like = jax.ShapeDtypeStruct(image.shape, jnp.float32)
    return pl.pallas_call(
        ritz_kernel,
        in_specs=[vmem] * 4,
        out_specs=[vmem] * 3,
        out_shape=[like, like, jax.ShapeDtypeStruct(gram.shape, jnp.float32)],
        compiler_params=pltpu.CompilerParams(vmem_limit_bytes=40 << 20),
    )(gram, projected, basis, image)


def local(tiles, tile_rows, tile_cols, tile_counts, block_x, block_p):
    tile_block = tiles[0, 0]
    rows = tile_rows[0, 0]
    cols = tile_cols[0, 0]
    edge = tile_block.shape[-1]
    panel_tiles = block_x.shape[1] // edge
    diag_index = lax.axis_index("diag")
    long_index = lax.axis_index("long")
    long_size = lax.axis_size("long")
    diag_size = lax.axis_size("diag")
    folded = long_index < 2 * diag_index
    row_panel = jnp.where(folded, long_size - 1 - long_index, long_index)
    segment_id = jnp.where(folded, diag_size - 1 - diag_index, diag_index)
    meta = jnp.stack(
        [tile_counts[0, 0], row_panel * panel_tiles, 2 * segment_id * panel_tiles]
    ).astype(jnp.int32)

    def apply_hamiltonian(vectors):
        whole = lax.all_gather(vectors, "long", axis=1, tiled=True)
        spread = apply_tiles(tile_block, rows, cols, meta, whole)
        total = lax.psum_scatter(spread, "long", scatter_dimension=1, tiled=True)
        return lax.psum(total, "diag")

    width = block_x.shape[0]
    first = apply_hamiltonian(jnp.concatenate([block_x, block_p], 0))
    image_x = first[:width]
    image_p = first[width:]
    block_float = block_x.astype(jnp.float32)
    numerator, denominator = lax.psum(
        (jnp.sum(block_float * image_x, axis=1), jnp.sum(block_float * block_float, axis=1)), "long"
    )
    quotient = numerator / denominator
    search = (image_x - quotient[:, None] * block_float).astype(jnp.bfloat16)
    image_w = apply_hamiltonian(search)
    basis_in = jnp.concatenate([block_x, search, block_p], 0)
    himage = jnp.concatenate([image_x, image_w, image_p], 0)
    basis_float = basis_in.astype(jnp.float32)
    gram, projected = lax.psum(
        (
            jnp.dot(basis_float, basis_float.T, precision=HIGHEST),
            jnp.dot(basis_float, himage.T, precision=HIGHEST),
        ),
        "long",
    )
    return tuple(ritz(gram, projected, basis_in, himage))


def solution(mesh):
    return jax.shard_map(
        local,
        mesh=mesh,
        in_specs=(
            P("diag", "long", None, None, None),
            P("diag", "long", None),
            P("diag", "long", None),
            P("diag", "long"),
            P(None, "long"),
            P(None, "long"),
        ),
        out_specs=(P(None, "long"), P(None, "long"), P()),
        check_vma=False,
    )
```

time: 516 us -> 313 us (0.61); the launches traced: 512 us -> 314 us
  other arithmetic: 189 us -> 4.89 us
  matrix products: 59.5 us -> 1.55 us
  Pallas kernels: 0 us -> 43.4 us
  waiting for transfers between devices: 187 us -> 202 us
  local copies, waits for them, and re-layouts: 16.6 us -> 2.78 us
    scatter-add x4 -> x0, other arithmetic: 171 us -> none  [the longest x2 85.9 us: apply_hamiltonian(): row_part = jnp.zeros((count_vec, panel_tiles, edge), jnp.float32).at[:, r...]
    dot_general x10 -> x2, matrix products: 59.2 us -> 1.55 us  [the longest x1 1.34 us: local(): jnp.dot(basis_float, himage.T, precision=HIGHEST)]
    pallas_call x0 -> x3, Pallas kernels: none -> 43.4 us  [the longest x2 37.1 us: apply_tiles(): pl.pallas_call(tile_kernel, grid=(slots // STEP,), in_specs=[smem, smem,...]
    reduce_scatter x2, waiting for transfers between devices: 83.8 us -> 96.7 us  [apply_hamiltonian(): total = lax.psum_scatter(spread, 'long', scatter_dimension=1, tiled=True)]
    gather x4 -> x0, local copies, waits for them, and re-layouts: 11 us -> none  [the longest x2 5.51 us: apply_hamiltonian(): jnp.take(own_tiles, rows, axis=1)]
    another operation x5 -> x1, other arithmetic: 9.38 us -> 0.08 us  [local(): jnp.stack([tile_counts[0, 0], row_panel * panel_tiles, 2 * segment_id * p...]
where the time goes in v1:
time: 313 us; the launch traced here: 314 us
  waiting for transfers between devices  202 us (65%)
  blocking collectives  44.7 us (14%)
  Pallas kernels  43.4 us (14%)
  between operations  14.5 us (5%)
  other arithmetic  4.89 us (2%)
    reduce_scatter x2, waiting for transfers between devices, apply_hamiltonian(): total = lax.psum_scatter(spread, 'long', scatter_dimension=1, tiled=True)  96.7 us
    psum x2, waiting for transfers between devices, apply_hamiltonian(): return lax.psum(total, 'diag')  76.3 us
    pallas_call x2, Pallas kernels, apply_tiles(): pl.pallas_call(tile_kernel, grid=(slots // STEP,), in_specs=[smem, smem,...  37.1 us
    all_gather x1, waiting for transfers between devices, apply_hamiltonian(): whole = lax.all_gather(vectors, 'long', axis=1, tiled=True)  29.2 us
    psum x1, blocking collectives, local(): lax.psum((jnp.dot(basis_float, basis_float.T, precision=HIGHEST), jnp.dot...  22.7 us
    psum x1, blocking collectives, local(): lax.psum((jnp.sum(block_float * image_x, axis=1), jnp.sum(block_float * b...  11.9 us
    all_gather x1, blocking collectives, apply_hamiltonian(): whole = lax.all_gather(vectors, 'long', axis=1, tiled=True)  10.1 us
    pallas_call x1, Pallas kernels, ritz(): pl.pallas_call(ritz_kernel, in_specs=[vmem] * 4, out_specs=[vmem] * 3, ou...  6.36 us
  transfers between devices with their start and end apart: 5, of which 5 were waited for; matrix products, arithmetic and copies ran while one was open for 0% of the time, Pallas kernels for 0%

profile of v1, /device:TPU:0, one launch (start us, length us, event | category | flops | bytes accessed | tf_op | source)
XLA Modules:
  0.0 314.4 jit_solution(16012407607354347295)
XLA Ops:
  7.2 0.0 all-gather.2.cloned.1.call-start
  7.2 1.6 pad_maximum_fusion.2
  8.8 0.0 all-gather.2.cloned.1.call-update
  8.9 0.0 reduce-scatter.3.cloned.1.call-start
  9.6 0.1 pad_add_fusion.meta_ref
  9.7 29.2 %all-gather.2.cloned.1.call-done.vec_ref = bf16[32,24576]{1,0:T(8,128)(2,1)} async-done(((bf16[32,3072]{1,0:T(8,128)(2,1)}), bf16[32,24576]{1,0:T(8,128)(2,1)}) %all-gather.2.cloned.1.call-update) | async-done | bytes 1572880 | tf_op jit(solution)/shard_map/all_gather | solution.py:137
  38.9 0.0 copy-start
  38.9 1.4 copy-done
  40.3 0.0 copy-start.1
  40.3 0.7 copy-done.1
  41.0 0.0 copy-start.3
  41.0 0.7 copy-done.3
  41.7 18.8 %shard_map.85 = f32[32,24576]{1,0:T(8,128)} custom-call(s32[512]{0:T(512)S(1)} %bitcast.10, s32[512]{0:T(512)S(1)} %bitcast.12, s32[3]{0:T(128)S(1)} %pad_add_fusion.meta_ref, bf16[32,24576]{1,0:T(8,128)(2,1)S(1)} %copy-done, bf16[512,128,128]{2,1,0:T(8,128)(2,1)} %bitcast.14), custom_call_target="tpu_custom_call" | custom-call | flops 1073741824 | bytes 16777216 | tf_op jit(solution)/shard_map/pallas_call | solution.py:57
  60.5 0.0 copy-start.5
  60.5 0.0 copy-start.2
  60.5 0.0 copy-start.4
  60.5 0.0 reduce-scatter.3.cloned.1.call-update
  60.5 0.0 all-reduce.5.cloned.1.call-start
  60.6 52.8 %reduce-scatter.3.cloned.1.call-done = f32[32,3072]{1,0:T(8,128)} async-done(((f32[32,24576]{1,0:T(8,128)}), f32[32,3072]{1,0:T(8,128)}) %reduce-scatter.3.cloned.1.call-update) | async-done | bytes 393232 | tf_op jit(solution)/shard_map/reduce_scatter | solution.py:139
  113.4 0.0 all-reduce.5.cloned.1.call-update
  113.5 0.0 reduce-scatter.5.cloned.1.call-start
  113.5 39.5 %all-reduce.5.cloned.1.call-done = f32[32,3072]{1,0:T(8,128)} async-done(((f32[32,3072]{1,0:T(8,128)}), f32[32,3072]{1,0:T(8,128)}) %all-reduce.5.cloned.1.call-update) | async-done | bytes 393232 | tf_op jit(solution)/shard_map/psum | solution.py:140
  153.0 0.0 copy-done.5
  153.0 1.2 fusion.1
  154.2 11.9 %all-reduce.1 = (f32[16]{0:T(128)S(1)}, f32[16]{0:T(128)S(1)}) all-reduce(f32[16]{0:T(128)S(1)} %get-tuple-element.4, f32[16]{0:T(128)S(1)} %get-tuple-element.3), channel_id=1, replica_groups=mesh['diag'=4,'long'=8] {'long'}, use_global_device_ids=true, to_apply=%region_3.4 | all-reduce | flops 32 | bytes 256 | tf_op jit(solution)/shard_map/psum | solution.py:147
  166.1 1.0 fusion.3
  167.1 10.1 %all_gather.7.vec_ref = bf16[16,24576]{1,0:T(8,128)(2,1)S(1)} all-gather(bf16[16,3072]{1,0:T(8,128)(2,1)S(1)} %fusion.3), channel_id=1, replica_groups=mesh['diag'=4,'long'=8] {'long'}, dimensions={1}, use_global_device_ids=true | all-gather | bytes 884736 | tf_op jit(solution)/shard_map/all_gather | solution.py:137
  177.2 0.0 copy-done.2
  177.2 0.0 copy-done.4
  177.2 0.0 copy-start.6
  177.2 18.2 %shard_map.86 = f32[16,24576]{1,0:T(8,128)} custom-call(s32[512]{0:T(512)S(1)} %bitcast.11, s32[512]{0:T(512)S(1)} %bitcast.13, s32[3]{0:T(128)S(1)} %pad_add_fusion.meta_ref, bf16[16,24576]{1,0:T(8,128)(2,1)S(1)} %all_gather.7.vec_ref, bf16[512,128,128]{2,1,0:T(8,128)(2,1)} %bitcast.15), custom_call_target="tpu_custom_call" | custom-call | flops 536870912 | bytes 16777216 | tf_op jit(solution)/shard_map/pallas_call | solution.py:57
  195.4 0.0 reduce-scatter.5.cloned.1.call-update
  195.4 0.0 all-reduce.7.cloned.1.call-start
  195.5 0.0 copy-done.6
  195.5 43.9 %reduce-scatter.5.cloned.1.call-done = f32[16,3072]{1,0:T(8,128)} async-done(((f32[16,24576]{1,0:T(8,128)}), f32[16,3072]{1,0:T(8,128)}) %reduce-scatter.5.cloned.1.call-update) | async-done | bytes 196624 | tf_op jit(solution)/shard_map/reduce_scatter | solution.py:139
  239.4 0.0 all-reduce.7.cloned.1.call-update
  239.5 0.2 fusion.5
  239.7 36.8 %all-reduce.7.cloned.1.call-done = f32[16,3072]{1,0:T(8,128)} async-done(((f32[16,3072]{1,0:T(8,128)}), f32[16,3072]{1,0:T(8,128)}) %all-reduce.7.cloned.1.call-update) | async-done | bytes 196624 | tf_op jit(solution)/shard_map/psum | solution.py:140
  276.4 1.3 fusion.4
  277.8 22.7 %all-reduce = (f32[48,48]{1,0:T(8,128)S(1)}, f32[48,48]{1,0:T(8,128)S(1)}) all-reduce(f32[48,48]{1,0:T(8,128)S(1)} %fusion.5, f32[48,48]{1,0:T(8,128)S(1)} %fusion.4), channel_id=1, replica_groups=mesh['diag'=4,'long'=8] {'long'}, use_global_device_ids=true, to_apply=%region_6.7 | all-reduce | flops 4608 | bytes 36864 | tf_op jit(solution)/shard_map/psum | solution.py:156
  300.5 1.0 pad_maximum_fusion.image_ref
  301.5 6.4 %shard_map.87 = (f32[48,3072]{1,0:T(8,128)}, f32[48,3072]{1,0:T(8,128)}, f32[48,48]{1,0:T(8,128)}) custom-call(f32[48,48]{1,0:T(8,128)S(1)} %get-tuple-element.5.gram_ref, f32[48,48]{1,0:T(8,128)S(1)} %get-tuple-element.6.proj_ref, bf16[48,3072]{1,0:T(8,128)(2,1)S(1)} %pad_maximum_fusion.1.basis_ref, f32[48,3072]{1,0:T(8,128)S(1)} %pad_maximum_fusion.image_ref), custom_call_target="tpu_custom_call" | custom-call | tf_op jit(solution)/shard_map/pallas_call | solution.py:110
  (2 shorter events, 0.0 us)
Async XLA Ops:
  7.2 31.7 %all-gather.2.cloned.1.call-start = ((), (), s32[]{:S(2)}) async-start(), calls=%async_computation.2 | async-start | bytes 1769472 | tf_op jit(solution)/shard_map/all_gather | solution.py:137
  8.9 104.6 %reduce-scatter.3.cloned.1.call-start = ((), (), s32[]{:S(2)}) async-start(), calls=%async_computation.3 | async-start | bytes 3538944 | tf_op jit(solution)/shard_map/reduce_scatter | solution.py:139
  38.9 1.4 copy-start
  40.3 0.7 copy-start.1
  41.0 0.7 copy-start.3
  60.5 92.5 %copy-start.5 = (bf16[16,3072]{1,0:T(8,128)(2,1)S(1)}, bf16[16,3072]{1,0:T(8,128)(2,1)}, u32[]{:S(2)}) copy-start(bf16[16,3072]{1,0:T(8,128)(2,1)} %param.10) | copy-start | bytes 294916
  60.5 116.7 %copy-start.2 = (s32[1,1,512]{2,1,0:T(1,128)S(1)}, s32[1,1,512]{2,1,0:T(1,128)}, u32[]{:S(2)}) copy-start(s32[1,1,512]{2,1,0:T(1,128)} %param.7) | copy-start | bytes 6148
  60.5 116.7 %copy-start.4 = (s32[1,1,512]{2,1,0:T(1,128)S(1)}, s32[1,1,512]{2,1,0:T(1,128)}, u32[]{:S(2)}) copy-start(s32[1,1,512]{2,1,0:T(1,128)} %param.8) | copy-start | bytes 6148
  60.5 92.4 %all-reduce.5.cloned.1.call-start = ((), (), s32[]{:S(2)}) async-start(), calls=%async_computation.4 | async-start | bytes 786432 | tf_op jit(solution)/shard_map/psum | solution.py:140
  113.5 126.0 %reduce-scatter.5.cloned.1.call-start = ((), (), s32[]{:S(2)}) async-start(), calls=%async_computation.5 | async-start | bytes 1769472 | tf_op jit(solution)/shard_map/reduce_scatter | solution.py:139
  177.2 18.3 %copy-start.6 = (bf16[16,3072]{1,0:T(8,128)(2,1)S(1)}, bf16[16,3072]{1,0:T(8,128)(2,1)}, u32[]{:S(2)}) copy-start(bf16[16,3072]{1,0:T(8,128)(2,1)} %param.11) | copy-start | bytes 294916
  195.4 81.0 %all-reduce.7.cloned.1.call-start = ((), (), s32[]{:S(2)}) async-start(), calls=%async_computation.6 | async-start | bytes 393216 | tf_op jit(solution)/shard_map/psum | solution.py:140
Sparse Core Ops, SparseCore 0:
  10.5 28.3 all-gather.1
  60.7 52.7 reduce-scatter.2
  115.9 37.0 all-reduce.4
  195.6 43.8 reduce-scatter.4
  241.6 34.7 all-reduce.6

commit v2 on v1

--- a/solution.py
+++ b/solution.py
@@ -14,6 +14,7 @@
 
 def tile_kernel(rows_ref, cols_ref, meta_ref, vec_ref, tile_ref, out_ref):
     edge = tile_ref.shape[-1]
+    row_lane = out_ref.shape[1] // 3 * 2
     base = pl.program_id(0) * STEP
 
     @pl.when(pl.program_id(0) == 0)
@@ -27,11 +28,11 @@
         spots = []
         for u in range(UNROLL):
             k = i * UNROLL + u
-            row = rows_ref[base + k] + row_off
-            col = cols_ref[base + k] + col_off
-            weight = jnp.where(row == col, 0.5, 1.0).astype(jnp.float32)
+            row = rows_ref[base + k]
+            col = cols_ref[base + k]
+            weight = jnp.where(row + row_off == col + col_off, 0.5, 1.0).astype(jnp.float32)
             weight = jnp.where(base + k < count, weight, 0.0)
-            row_at = pl.ds(pl.multiple_of(row * edge, edge), edge)
+            row_at = pl.ds(pl.multiple_of(row * edge + row_lane, edge), edge)
             col_at = pl.ds(pl.multiple_of(col * edge, edge), edge)
             tile = tile_ref[k]
             forward = lax.dot_general(
@@ -75,12 +76,13 @@
     )(rows, cols, meta, vectors, tiles)
 
 
-def ritz_kernel(gram_ref, proj_ref, basis_ref, image_ref, rb_ref, ri_ref, rm_ref):
-    size = gram_ref.shape[0]
+def ritz_kernel(sums_ref, basis_ref, image_ref, rb_ref, ri_ref, rm_ref):
+    size = sums_ref.shape[0]
     lane = lax.broadcasted_iota(jnp.int32, (size, size), 1)
     row = lax.broadcasted_iota(jnp.int32, (size, size), 0)
     below = lax.broadcasted_iota(jnp.int32, (size, 1), 0)
-    left = gram_ref[...]
+    sums = sums_ref[...]
+    left = sums[:, :size]
     right = jnp.where(lane == row, 1.0, 0.0).astype(jnp.float32)
     pivots = jnp.zeros((size, 1), jnp.float32)
     for k in range(size):
@@ -92,7 +94,7 @@
         right = right - scale * right_row
     inverse = right * (1.0 / jnp.sqrt(pivots))
     nt = (((1,), (1,)), ((), ()))
-    half = jnp.dot(inverse, proj_ref[...], precision=HIGHEST, preferred_element_type=jnp.float32)
+    half = jnp.dot(inverse, sums[:, size : 2 * size], precision=HIGHEST, preferred_element_type=jnp.float32)
     one = lax.dot_general(half, inverse, nt, precision=HIGHEST, preferred_element_type=jnp.float32)
     two = lax.dot_general(inverse, half, nt, precision=HIGHEST, preferred_element_type=jnp.float32)
     rm_ref[...] = 0.5 * (one + two)
@@ -104,16 +106,329 @@
     )
 
 
-def ritz(gram, projected, basis, image):
+def ritz(sums, basis, image):
     vmem = pl.BlockSpec(memory_space=pltpu.VMEM)
     like = jax.ShapeDtypeStruct(image.shape, jnp.float32)
     return pl.pallas_call(
         ritz_kernel,
-        in_specs=[vmem] * 4,
+        in_specs=[vmem] * 3,
         out_specs=[vmem] * 3,
-        out_shape=[like, like, jax.ShapeDtypeStruct(gram.shape, jnp.float32)],
+        out_shape=[like, like, jax.ShapeDtypeStruct((sums.shape[0], sums.shape[0]), jnp.float32)],
         compiler_params=pltpu.CompilerParams(vmem_limit_bytes=40 << 20),
-    )(gram, projected, basis, image)
+    )(sums, basis, image)
+
+
+class Place:
+    def __init__(self, diag_size, long_size):
+        self.diag_size, self.long_size = diag_size, long_size
+        self.chips = long_size // 2
+        self.d = lax.axis_index("diag")
+        self.c = lax.axis_index("long")
+        self.q, self.k = self.c // 2, self.c % 2
+        self.partner = self.q * 2 + 1 - self.k
+        self.mirror = long_size - 1 - self.c
+        self.folded = self.q < self.d
+        self.segment = self.segment_of(self.q)
+        self.mirror_folded = self.mirror // 2 < self.d
+
+    def segment_of(self, chip):
+        return jnp.where(chip < self.d, self.diag_size - 1 - self.d, self.d)
+
+    def copy(self, src, dst, send, recv, d, c):
+        return pltpu.make_async_remote_copy(
+            src_ref=src,
+            dst_ref=dst,
+            send_sem=send,
+            recv_sem=recv,
+            device_id=(d, c),
+            device_id_type=pl.DeviceIdType.MESH,
+        )
+
+    def enter(self):
+        barrier = pltpu.get_barrier_semaphore()
+        peers = [(self.d, (self.c + o) % self.long_size) for o in range(1, self.long_size)]
+        peers += [((self.d + o) % self.diag_size, self.c) for o in range(1, self.diag_size)]
+        for peer in peers:
+            pl.semaphore_signal(barrier, inc=1, device_id=peer, device_id_type=pl.DeviceIdType.MESH)
+        pl.semaphore_wait(barrier, len(peers))
+
+
+def spread_panels(at, own, vec, send, recv):
+    def to_chip(t):
+        return at.copy(own, vec.at[at.k], send.at[t], recv.at[0], at.d, 2 * t + at.k)
+
+    def wanted(t):
+        return jnp.logical_and(at.q != t, at.segment_of(t) == at.q)
+
+    mirror = at.copy(own, vec.at[2], send.at[at.chips], recv.at[1], at.d, at.mirror)
+    for t in range(at.chips):
+        @pl.when(wanted(t))
+        def _():
+            to_chip(t).start()
+
+    @pl.when(at.mirror_folded)
+    def _():
+        mirror.start()
+
+    pair = at.copy(
+        vec.at[at.k], vec.at[at.k], send.at[at.chips + 1], recv.at[2], at.d, at.partner
+    )
+
+    @pl.when(at.segment == at.q)
+    def _():
+        vec[at.k] = own[...]
+
+    @pl.when(at.segment != at.q)
+    def _():
+        at.copy(own, vec.at[at.k], send.at[0], recv.at[0], at.d, at.partner).wait_recv()
+
+    pair.start()
+
+    @pl.when(at.folded)
+    def _():
+        mirror.wait_recv()
+
+    @pl.when(jnp.logical_not(at.folded))
+    def _():
+        vec[2] = own[...]
+
+    pair.wait()
+    for t in range(at.chips):
+        @pl.when(wanted(t))
+        def _():
+            to_chip(t).wait_send()
+
+    @pl.when(at.mirror_folded)
+    def _():
+        mirror.wait_send()
+
+
+def sum_slices(at, part, other, colsum, cols, rows, total, slots, send, recv):
+    states = other.shape[1]
+    width = total.shape[2]
+    pair = at.copy(
+        part.at[:, pl.ds(pl.multiple_of((1 - at.k) * states, 128), states)],
+        other, send.at[0], recv.at[0], at.d, at.partner,
+    )
+    mirror = at.copy(
+        part.at[:, pl.ds(2 * states, states)], rows, send.at[1], recv.at[1], at.d, at.mirror
+    )
+    home = at.copy(
+        colsum, cols.at[at.q], send.at[2], recv.at[2 + at.q], at.d, 2 * at.segment + at.k
+    )
+    pair.start()
+
+    @pl.when(at.folded)
+    def _():
+        mirror.start()
+
+    keep = jnp.where(at.folded, 0.0, 1.0).astype(jnp.float32)
+    for z in range(at.diag_size):
+        lanes = slice(2 * states + z * width, 2 * states + (z + 1) * width)
+        total[z] = part[:, lanes] * keep
+    pair.wait_recv()
+    colsum[...] = (
+        part[:, pl.ds(pl.multiple_of(at.k * states, 128), states)] + other[...]
+    )
+
+    @pl.when(at.segment != at.q)
+    def _():
+        home.start()
+
+    def add(panel):
+        for z in range(at.diag_size):
+            total[z] += panel[:, z * width : (z + 1) * width]
+
+    @pl.when(at.segment == at.q)
+    def _():
+        add(colsum)
+
+    @pl.when(at.mirror_folded)
+    def _():
+        mirror.wait_recv()
+        add(rows)
+
+    for t in range(at.chips):
+        @pl.when(jnp.logical_and(at.q != t, at.segment_of(t) == at.q))
+        def _():
+            at.copy(
+                colsum, cols.at[t], send.at[2], recv.at[2 + t], at.d, at.partner
+            ).wait_recv()
+            add(cols.at[t])
+
+    base = 2 + at.chips
+    moves = []
+    for o in range(1, at.diag_size):
+        peer = (at.d + o) % at.diag_size
+        moves.append(
+            at.copy(
+                total.at[peer], slots.at[o - 1], send.at[2 + o], recv.at[base + o - 1], peer, at.c
+            )
+        )
+        moves[-1].start()
+    value = total[at.d]
+    for o, move in enumerate(moves):
+        move.wait_recv()
+        value = value + slots[o]
+    for move in moves:
+        move.wait_send()
+    pair.wait_send()
+
+    @pl.when(at.folded)
+    def _():
+        mirror.wait_send()
+
+    @pl.when(at.segment != at.q)
+    def _():
+        home.wait_send()
+
+    return value
+
+
+def along_diag(at, slots, send, recv):
+    moves = []
+    for o in range(1, at.diag_size):
+        peer = (at.d + o) % at.diag_size
+        source = (at.d + at.diag_size - o) % at.diag_size
+        out = at.copy(slots.at[at.d], slots.at[at.d], send.at[o - 1], recv.at[o - 1], peer, at.c)
+        out.start()
+        into = at.copy(
+            slots.at[source], slots.at[source], send.at[o - 1], recv.at[o - 1], peer, at.c
+        )
+        moves.append((out, into))
+    return moves
+
+
+def along_long(at, slots, send, recv):
+    moves = []
+    for o in range(1, at.long_size):
+        peer = (at.c + o) % at.long_size
+        source = (at.c + at.long_size - o) % at.long_size
+        out = at.copy(slots.at[at.c], slots.at[at.c], send.at[o - 1], recv.at[o - 1], at.d, peer)
+        out.start()
+        into = at.copy(
+            slots.at[source], slots.at[source], send.at[o - 1], recv.at[o - 1], at.d, peer
+        )
+        moves.append((out, into))
+    return moves
+
+
+def finish(moves):
+    for _, into in moves:
+        into.wait_recv()
+    for out, _ in moves:
+        out.wait_send()
+
+
+def sum_all(at, value, by_diag, by_long, sems):
+    by_diag[at.d] = value
+    finish(along_diag(at, by_diag, sems[0], sems[1]))
+    value = by_diag[0]
+    for z in range(1, at.diag_size):
+        value = value + by_diag[z]
+    by_long[at.c] = value
+    finish(along_long(at, by_long, sems[2], sems[3]))
+    value = by_long[0]
+    for z in range(1, at.long_size):
+        value = value + by_long[z]
+    return value
+
+
+def gather_kernel(sizes, x_ref, p_ref, out_ref, own, vec, send, recv):
+    at = Place(*sizes)
+    at.enter()
+    count, states = x_ref.shape
+    own[:count] = x_ref[...]
+    own[count:] = p_ref[...]
+    spread_panels(at, own, vec, send, recv)
+    for i in range(3):
+        out_ref[:, i * states : (i + 1) * states] = vec[i]
+
+
+def search_kernel(
+    sizes, part, x_ref, slice_ref, search_ref, out_ref,
+    other, colsum, cols, rows, total, slots, by_diag, by_long, pieces, own, vec,
+    sum_send, sum_recv, z_send, z_recv, l_send, l_recv, s_send, s_recv, g_send, g_recv,
+):
+    at = Place(*sizes)
+    at.enter()
+    image = sum_slices(at, part, other, colsum, cols, rows, total, slots, sum_send, sum_recv)
+    slice_ref[...] = image
+    count, states = x_ref.shape
+    width = image.shape[1]
+    image = image[:count]
+    block = x_ref[:, pl.ds(pl.multiple_of(at.d * width, 128), width)].astype(jnp.float32)
+    both = jnp.concatenate([block * image, block * block], 0)
+    folded = both[:, :128]
+    for i in range(1, width // 128):
+        folded = folded + both[:, i * 128 : (i + 1) * 128]
+    sums = sum_all(at, folded, by_diag, by_long, (z_send, z_recv, l_send, l_recv))
+    sums = jnp.sum(sums, axis=1, keepdims=True)
+    quotient = sums[:count] / sums[count:]
+    pieces[at.d] = (image - quotient * block).astype(jnp.bfloat16)
+    finish(along_diag(at, pieces, s_send, s_recv))
+    for z in range(at.diag_size):
+        own[:, z * width : (z + 1) * width] = pieces[z]
+    spread_panels(at, own, vec, g_send, g_recv)
+    search_ref[...] = own[...]
+    for i in range(3):
+        out_ref[:, i * states : (i + 1) * states] = vec[i]
+
+
+def project_kernel(
+    sizes, part, first_ref, x_ref, search_ref, p_ref, sums_ref, image_ref,
+    other, colsum, cols, rows, total, slots, by_diag, by_long, pieces, both,
+    sum_send, sum_recv, z_send, z_recv, l_send, l_recv, s_send, s_recv,
+):
+    at = Place(*sizes)
+    at.enter()
+    image = sum_slices(at, part, other, colsum, cols, rows, total, slots, sum_send, sum_recv)
+    count, width = image.shape
+    pieces[at.d] = image
+    moves = along_diag(at, pieces, s_send, s_recv)
+    lanes = pl.ds(pl.multiple_of(at.d * width, 128), width)
+    both[:count] = x_ref[:, lanes].astype(jnp.float32)
+    both[count : 2 * count] = search_ref[:, lanes].astype(jnp.float32)
+    both[2 * count : 3 * count] = p_ref[:, lanes].astype(jnp.float32)
+    both[3 * count : 4 * count] = first_ref[:count]
+    both[4 * count : 5 * count] = image
+    both[5 * count : 6 * count] = first_ref[count:]
+    both[6 * count :] = jnp.zeros((both.shape[0] - 6 * count, width), jnp.float32)
+    value = lax.dot_general(
+        both[: 3 * count], both[...], (((1,), (1,)), ((), ())),
+        precision=HIGHEST, preferred_element_type=jnp.float32,
+    )
+    sums_ref[...] = sum_all(at, value, by_diag, by_long, (z_send, z_recv, l_send, l_recv))
+    finish(moves)
+    for z in range(at.diag_size):
+        image_ref[:, z * width : (z + 1) * width] = pieces[z]
+
+
+def sum_scratch(count, states, diag_size, long_size):
+    width = states // diag_size
+    f32 = jnp.float32
+    return [
+        pltpu.VMEM((count, states), f32),
+        pltpu.VMEM((count, states), f32),
+        pltpu.VMEM((long_size // 2, count, states), f32),
+        pltpu.VMEM((count, states), f32),
+        pltpu.VMEM((diag_size, count, width), f32),
+        pltpu.VMEM((diag_size - 1, count, width), f32),
+    ]
+
+
+def remote_call(kernel, sizes, collective, outs, scratch, *args):
+    vmem = pl.BlockSpec(memory_space=pltpu.VMEM)
+    return pl.pallas_call(
+        functools.partial(kernel, sizes),
+        in_specs=[vmem] * len(args),
+        out_specs=[vmem] * len(outs),
+        out_shape=[jax.ShapeDtypeStruct(*o) for o in outs],
+        scratch_shapes=scratch,
+        compiler_params=pltpu.CompilerParams(
+            collective_id=collective, has_side_effects=True, vmem_limit_bytes=40 << 20
+        ),
+    )(*args)
 
 
 def local(tiles, tile_rows, tile_cols, tile_counts, block_x, block_p):
@@ -121,7 +436,8 @@
     rows = tile_rows[0, 0]
     cols = tile_cols[0, 0]
     edge = tile_block.shape[-1]
-    panel_tiles = block_x.shape[1] // edge
+    count, states = block_x.shape
+    panel_tiles = states // edge
     diag_index = lax.axis_index("diag")
     long_index = lax.axis_index("long")
     long_size = lax.axis_size("long")
@@ -132,35 +448,54 @@
     meta = jnp.stack(
         [tile_counts[0, 0], row_panel * panel_tiles, 2 * segment_id * panel_tiles]
     ).astype(jnp.int32)
-
-    def apply_hamiltonian(vectors):
-        whole = lax.all_gather(vectors, "long", axis=1, tiled=True)
-        spread = apply_tiles(tile_block, rows, cols, meta, whole)
-        total = lax.psum_scatter(spread, "long", scatter_dimension=1, tiled=True)
-        return lax.psum(total, "diag")
-
-    width = block_x.shape[0]
-    first = apply_hamiltonian(jnp.concatenate([block_x, block_p], 0))
-    image_x = first[:width]
-    image_p = first[width:]
-    block_float = block_x.astype(jnp.float32)
-    numerator, denominator = lax.psum(
-        (jnp.sum(block_float * image_x, axis=1), jnp.sum(block_float * block_float, axis=1)), "long"
-    )
-    quotient = numerator / denominator
-    search = (image_x - quotient[:, None] * block_float).astype(jnp.bfloat16)
-    image_w = apply_hamiltonian(search)
+    sizes = (diag_size, long_size)
+    width = states // diag_size
+    chips = long_size // 2
+    f32, bf16, dma = jnp.float32, jnp.bfloat16, pltpu.SemaphoreType.DMA
+    spread_sems = [dma((chips + 2,)), dma((3,))]
+    sum_sems = [dma((diag_size + 2,)), dma((1 + chips + diag_size,))]
+    all_sems = [dma((n - 1,)) for n in (diag_size, diag_size, long_size, long_size)]
+    diag_sems = [dma((diag_size - 1,))] * 2
+
+    vectors = remote_call(
+        gather_kernel, sizes, 1, [((2 * count, 3 * states), bf16)],
+        [pltpu.VMEM((2 * count, states), bf16), pltpu.VMEM((3, 2 * count, states), bf16)]
+        + spread_sems,
+        block_x, block_p,
+    )[0]
+    part = apply_tiles(tile_block, rows, cols, meta, vectors)
+    first, search, vectors = remote_call(
+        search_kernel, sizes, 2,
+        [((2 * count, width), f32), ((count, states), bf16), ((count, 3 * states), bf16)],
+        sum_scratch(2 * count, states, *sizes)
+        + [
+            pltpu.VMEM((diag_size, 2 * count, 128), f32),
+            pltpu.VMEM((long_size, 2 * count, 128), f32),
+            pltpu.VMEM((diag_size, count, width), bf16),
+            pltpu.VMEM((count, states), bf16),
+            pltpu.VMEM((3, count, states), bf16),
+        ]
+        + sum_sems + all_sems + diag_sems + spread_sems,
+        part, block_x,
+    )
+    first_whole = lax.all_gather(first, "diag", axis=1, tiled=True)
+    part = apply_tiles(tile_block, rows, cols, meta, vectors)
+    sums, image_w = remote_call(
+        project_kernel, sizes, 3,
+        [((3 * count, 128), f32), ((count, states), f32)],
+        sum_scratch(count, states, *sizes)
+        + [
+            pltpu.VMEM((diag_size, 3 * count, 128), f32),
+            pltpu.VMEM((long_size, 3 * count, 128), f32),
+            pltpu.VMEM((diag_size, count, width), f32),
+            pltpu.VMEM((128, width), f32),
+        ]
+        + sum_sems + all_sems + diag_sems,
+        part, first, block_x, search, block_p,
+    )
     basis_in = jnp.concatenate([block_x, search, block_p], 0)
-    himage = jnp.concatenate([image_x, image_w, image_p], 0)
-    basis_float = basis_in.astype(jnp.float32)
-    gram, projected = lax.psum(
-        (
-            jnp.dot(basis_float, basis_float.T, precision=HIGHEST),
-            jnp.dot(basis_float, himage.T, precision=HIGHEST),
-        ),
-        "long",
-    )
-    return tuple(ritz(gram, projected, basis_in, himage))
+    himage = jnp.concatenate([first_whole[:count], image_w, first_whole[count:]], 0)
+    return tuple(ritz(sums, basis_in, himage))
 
 
 def solution(mesh):

time: 313 us -> 164 us (0.52)
  waiting for transfers between devices: 202 us -> 0 us
  Pallas kernels: 43.4 us -> 144 us
  blocking collectives: 44.7 us -> 14.3 us
  between operations: 14.5 us -> 1.41 us
  other arithmetic: 4.89 us -> 0.14 us
    pallas_call x1 -> x4, Pallas kernels: 6.36 us -> 110 us  [the longest x3 104 us: remote_call(): pl.pallas_call(functools.partial(kernel, sizes), in_specs=[vmem] * len(ar...]
    reduce_scatter x2 -> x0, waiting for transfers between devices: 96.7 us -> none  [apply_hamiltonian(): total = lax.psum_scatter(spread, 'long', scatter_dimension=1, tiled=True)]
    psum x2 -> x0, waiting for transfers between devices: 76.3 us -> none  [apply_hamiltonian(): return lax.psum(total, 'diag')]
    psum x2 -> x0, blocking collectives: 34.6 us -> none  [the longest x1 22.7 us: local(): lax.psum((jnp.dot(basis_float, basis_float.T, precision=HIGHEST), jnp.dot...]
    all_gather x1 -> x0, waiting for transfers between devices: 29.2 us -> none  [apply_hamiltonian(): whole = lax.all_gather(vectors, 'long', axis=1, tiled=True)]
    all_gather x1, blocking collectives: 10.1 us -> 14.3 us  [local(): first_whole = lax.all_gather(first, 'diag', axis=1, tiled=True)]
  transfers between devices with their start and end apart: 5 -> 0, of which waited for: 5 -> 0; matrix products, arithmetic and copies ran while one was open for 0% -> 0% of each run, Pallas kernels for 0% -> 0%
where the time goes in v2:
time: 164 us; the launch traced here: 163 us
  Pallas kernels  144 us (88%)
  blocking collectives  14.3 us (9%)
  local copies, waits for them, and re-layouts  3.19 us (2%)
    pallas_call x3, Pallas kernels, remote_call(): pl.pallas_call(functools.partial(kernel, sizes), in_specs=[vmem] * len(ar...  104 us
    pallas_call x2, Pallas kernels, apply_tiles(): pl.pallas_call(tile_kernel, grid=(slots // STEP,), in_specs=[smem, smem,...  34 us
    all_gather x1, blocking collectives, local(): first_whole = lax.all_gather(first, 'diag', axis=1, tiled=True)  14.3 us
    pallas_call x1, Pallas kernels, ritz(): pl.pallas_call(ritz_kernel, in_specs=[vmem] * 3, out_specs=[vmem] * 3, ou...  6.38 us

profile of v2, /device:TPU:0, one launch (start us, length us, event | category | flops | bytes accessed | tf_op | source)
XLA Modules:
  0.0 163.3 jit_solution(17929264506757877569)
XLA Ops:
  0.6 0.0 copy-start.7
  0.6 0.0 copy-start.5
  1.3 0.1 pad_add_fusion.meta_ref
  1.4 0.0 copy-start
  1.4 0.9 copy-done
  2.3 0.0 copy-start.2
  2.3 0.9 copy-done.2
  3.2 13.6 %shard_map.85.vec_ref = bf16[32,9216]{1,0:T(8,128)(2,1)S(1)} custom-call(bf16[16,3072]{1,0:T(8,128)(2,1)S(1)} %copy-done, bf16[16,3072]{1,0:T(8,128)(2,1)S(1)} %copy-done.2), custom_call_target="tpu_custom_call" | custom-call | tf_op jit(solution)/shard_map/pallas_call | solution.py:422
  16.7 0.0 copy-start.4
  16.8 0.7 copy-done.4
  17.4 0.0 copy-start.6
  17.4 0.7 copy-done.6
  18.1 0.0 copy-start.1
  18.1 0.0 copy-start.3
  18.1 17.1 %shard_map.86.part = f32[32,9216]{1,0:T(8,128)S(1)} custom-call(s32[512]{0:T(512)S(1)} %bitcast.7, s32[512]{0:T(512)S(1)} %bitcast.9, s32[3]{0:T(128)S(1)} %pad_add_fusion.meta_ref, bf16[32,9216]{1,0:T(8,128)(2,1)S(1)} %shard_map.85.vec_ref, bf16[512,128,128]{2,1,0:T(8,128)(2,1)} %bitcast.11), custom_call_target="tpu_custom_call" | custom-call | flops 1073741824 | bytes 16777216 | tf_op jit(solution)/shard_map/pallas_call | solution.py:58
  35.2 52.6 %shard_map.87 = (f32[32,768]{1,0:T(8,128)S(1)}, bf16[16,3072]{1,0:T(8,128)(2,1)S(1)}, bf16[16,9216]{1,0:T(8,128)(2,1)S(1)}) custom-call(f32[32,9216]{1,0:T(8,128)S(1)} %shard_map.86.part, bf16[16,3072]{1,0:T(8,128)(2,1)S(1)} %copy-done), custom_call_target="tpu_custom_call" | custom-call | tf_op jit(solution)/shard_map/pallas_call | solution.py:422
  87.9 0.0 copy-done.7
  87.9 0.0 copy-done.5
  87.9 16.9 %shard_map.88.part = f32[16,9216]{1,0:T(8,128)S(1)} custom-call(s32[512]{0:T(512)S(1)} %bitcast.8, s32[512]{0:T(512)S(1)} %bitcast.10, s32[3]{0:T(128)S(1)} %pad_add_fusion.meta_ref, bf16[16,9216]{1,0:T(8,128)(2,1)S(1)} %get-tuple-element.8.vec_ref, bf16[512,128,128]{2,1,0:T(8,128)(2,1)} %bitcast.12), custom_call_target="tpu_custom_call" | custom-call | flops 536870912 | bytes 16777216 | tf_op jit(solution)/shard_map/pallas_call | solution.py:58
  104.8 0.0 copy-done.1
  104.8 0.0 copy-done.3
  104.8 37.6 %shard_map.89 = (f32[48,128]{1,0:T(8,128)S(1)}, f32[16,3072]{1,0:T(8,128)S(1)}) custom-call(f32[16,9216]{1,0:T(8,128)S(1)} %shard_map.88.part, f32[32,768]{1,0:T(8,128)S(1)} %get-tuple-element.9.first_ref, bf16[16,3072]{1,0:T(8,128)(2,1)S(1)} %copy-done.1, bf16[16,3072]{1,0:T(8,128)(2,1)S(1)} %get-tuple-element.10.search_ref, bf16[16,3072]{1,0:T(8,128)(2,1)S(1)} %copy-done.3), custom_call_target="tpu_custom_call" | custom-call | tf_op jit(solution)/shard_map/pallas_call | solution.py:422
  142.5 14.3 %all_gather.3 = f32[32,3072]{1,0:T(8,128)S(1)} all-gather(f32[32,768]{1,0:T(8,128)S(1)} %get-tuple-element.9.first_ref), channel_id=1, replica_groups=mesh['diag'=4,'long'=8] {'diag'}, dimensions={1}, use_global_device_ids=true | all-gather | bytes 491520 | tf_op jit(solution)/shard_map/all_gather | solution.py:481
  156.9 6.4 %shard_map.90 = (f32[48,3072]{1,0:T(8,128)}, f32[48,3072]{1,0:T(8,128)}, f32[48,48]{1,0:T(8,128)}) custom-call(f32[48,128]{1,0:T(8,128)S(1)} %get-tuple-element.11.sums_ref, bf16[48,3072]{1,0:T(8,128)(2,1)S(1)} %pad_maximum_fusion.1.basis_ref, f32[48,3072]{1,0:T(8,128)S(1)} %pad_maximum_fusion.image_ref), custom_call_target="tpu_custom_call" | custom-call | tf_op jit(solution)/shard_map/pallas_call | solution.py:112
  (3 shorter events, 0.1 us)
Async XLA Ops:
  0.6 87.2 %copy-start.7 = (s32[1,1,512]{2,1,0:T(1,128)S(1)}, s32[1,1,512]{2,1,0:T(1,128)}, u32[]{:S(2)}) copy-start(s32[1,1,512]{2,1,0:T(1,128)} %param.8) | copy-start | bytes 6148
  0.6 87.2 %copy-start.5 = (s32[1,1,512]{2,1,0:T(1,128)S(1)}, s32[1,1,512]{2,1,0:T(1,128)}, u32[]{:S(2)}) copy-start(s32[1,1,512]{2,1,0:T(1,128)} %param.7) | copy-start | bytes 6148
  1.4 0.9 copy-start
  2.3 0.9 copy-start.2
  16.7 0.7 copy-start.4
  17.4 0.7 copy-start.6
  18.1 86.7 %copy-start.1 = (bf16[16,3072]{1,0:T(8,128)(2,1)S(1)}, bf16[16,3072]{1,0:T(8,128)(2,1)}, u32[]{:S(2)}) copy-start(bf16[16,3072]{1,0:T(8,128)(2,1)} %x_ref.5) | copy-start | bytes 294916
  18.1 86.7 %copy-start.3 = (bf16[16,3072]{1,0:T(8,128)(2,1)S(1)}, bf16[16,3072]{1,0:T(8,128)(2,1)}, u32[]{:S(2)}) copy-start(bf16[16,3072]{1,0:T(8,128)(2,1)} %p_ref.3) | copy-start | bytes 294916

commit v3 on v2

--- a/solution.py
+++ b/solution.py
@@ -9,7 +9,7 @@
 
 HIGHEST = lax.Precision.HIGHEST
 STEP = 64
-UNROLL = 8
+UNROLL = 32
 
 
 def tile_kernel(rows_ref, cols_ref, meta_ref, vec_ref, tile_ref, out_ref):
@@ -24,26 +24,43 @@
     count, row_off, col_off = meta_ref[0], meta_ref[1], meta_ref[2]
     live = jnp.clip(count - base, 0, STEP)
 
+    count_vec = vec_ref.shape[0]
+    blank = jnp.zeros((count_vec, edge), vec_ref.dtype)
+
+    def spot(k):
+        row = rows_ref[base + k]
+        col = cols_ref[base + k]
+        weight = jnp.where(row + row_off == col + col_off, 0.5, 1.0).astype(jnp.float32)
+        weight = jnp.where(base + k < count, weight, 0.0)
+        row_at = pl.ds(pl.multiple_of(row * edge + row_lane, edge), edge)
+        col_at = pl.ds(pl.multiple_of(col * edge, edge), edge)
+        return row_at, col_at, weight
+
     def group(i, carry):
-        spots = []
-        for u in range(UNROLL):
+        found = []
+        for u in range(0, UNROLL, 2):
             k = i * UNROLL + u
-            row = rows_ref[base + k]
-            col = cols_ref[base + k]
-            weight = jnp.where(row + row_off == col + col_off, 0.5, 1.0).astype(jnp.float32)
-            weight = jnp.where(base + k < count, weight, 0.0)
-            row_at = pl.ds(pl.multiple_of(row * edge + row_lane, edge), edge)
-            col_at = pl.ds(pl.multiple_of(col * edge, edge), edge)
-            tile = tile_ref[k]
+            row_a, col_a, weight_a = spot(k)
+            row_b, col_b, weight_b = spot(k + 1)
+            two = tile_ref[pl.ds(k, 2)].reshape(2 * edge, edge)
             forward = lax.dot_general(
-                vec_ref[:, col_at],
-                tile,
+                jnp.concatenate([vec_ref[:, col_a], vec_ref[:, col_b]], 0),
+                two,
                 (((1,), (1,)), ((), ())),
                 preferred_element_type=jnp.float32,
             )
-            backward = jnp.dot(vec_ref[:, row_at], tile, preferred_element_type=jnp.float32)
-            spots.append((row_at, col_at, forward * weight, backward * weight))
-        for row_at, col_at, forward, backward in spots:
+            upper = jnp.concatenate([vec_ref[:, row_a], blank], 1)
+            lower = jnp.concatenate([blank, vec_ref[:, row_b]], 1)
+            backward = jnp.dot(
+                jnp.concatenate([upper, lower], 0), two, preferred_element_type=jnp.float32
+            )
+            found.append(
+                (row_a, col_a, forward[:count_vec, :edge] * weight_a, backward[:count_vec] * weight_a)
+            )
+            found.append(
+                (row_b, col_b, forward[count_vec:, edge:] * weight_b, backward[count_vec:] * weight_b)
+            )
+        for row_at, col_at, forward, backward in found:
             out_ref[:, row_at] += forward
             out_ref[:, col_at] += backward
         return carry
@@ -203,86 +220,104 @@
         mirror.wait_send()
 
 
-def sum_slices(at, part, other, colsum, cols, rows, total, slots, send, recv):
-    states = other.shape[1]
-    width = total.shape[2]
-    pair = at.copy(
-        part.at[:, pl.ds(pl.multiple_of((1 - at.k) * states, 128), states)],
-        other, send.at[0], recv.at[0], at.d, at.partner,
-    )
-    mirror = at.copy(
-        part.at[:, pl.ds(2 * states, states)], rows, send.at[1], recv.at[1], at.d, at.mirror
-    )
-    home = at.copy(
-        colsum, cols.at[at.q], send.at[2], recv.at[2 + at.q], at.d, 2 * at.segment + at.k
-    )
-    pair.start()
-
-    @pl.when(at.folded)
-    def _():
-        mirror.start()
-
-    keep = jnp.where(at.folded, 0.0, 1.0).astype(jnp.float32)
-    for z in range(at.diag_size):
-        lanes = slice(2 * states + z * width, 2 * states + (z + 1) * width)
-        total[z] = part[:, lanes] * keep
-    pair.wait_recv()
-    colsum[...] = (
-        part[:, pl.ds(pl.multiple_of(at.k * states, 128), states)] + other[...]
-    )
-
-    @pl.when(at.segment != at.q)
-    def _():
-        home.start()
-
-    def add(panel):
+class PanelSum:
+    def __init__(self, at, part, lo, hi, bufs, send, recv):
+        self.at, self.part, self.lo, self.hi = at, part, lo, hi
+        self.other, self.colsum, self.cols, self.rows, self.total, self.slots = bufs
+        self.send, self.recv = send, recv
+        self.states, self.width = self.other.shape[1], self.total.shape[2]
+        states = self.states
+        self.mine = pl.ds(pl.multiple_of(at.k * states, 128), states)
+        theirs = pl.ds(pl.multiple_of((1 - at.k) * states, 128), states)
+        self.pair = at.copy(
+            part.at[lo:hi, theirs], self.other, send.at[0], recv.at[0], at.d, at.partner
+        )
+        self.mirror = at.copy(
+            part.at[lo:hi, pl.ds(2 * states, states)],
+            self.rows, send.at[1], recv.at[1], at.d, at.mirror,
+        )
+        self.home = at.copy(
+            self.colsum, self.cols.at[at.q], send.at[2], recv.at[2 + at.q],
+            at.d, 2 * at.segment + at.k,
+        )
+
+    def start(self):
+        self.pair.start()
+
+        @pl.when(self.at.folded)
+        def _():
+            self.mirror.start()
+
+    def columns(self):
+        at = self.at
+        self.pair.wait_recv()
+        self.colsum[...] = self.part[self.lo : self.hi, self.mine] + self.other[...]
+
+        @pl.when(at.segment != at.q)
+        def _():
+            self.home.start()
+
+    def add(self, panel):
+        width = self.width
+        for z in range(self.at.diag_size):
+            self.total[z] += panel[:, z * width : (z + 1) * width]
+
+    def totals(self):
+        at, width = self.at, self.width
+        keep = jnp.where(at.folded, 0.0, 1.0).astype(jnp.float32)
         for z in range(at.diag_size):
-            total[z] += panel[:, z * width : (z + 1) * width]
-
-    @pl.when(at.segment == at.q)
-    def _():
-        add(colsum)
-
-    @pl.when(at.mirror_folded)
-    def _():
-        mirror.wait_recv()
-        add(rows)
-
-    for t in range(at.chips):
-        @pl.when(jnp.logical_and(at.q != t, at.segment_of(t) == at.q))
-        def _():
-            at.copy(
-                colsum, cols.at[t], send.at[2], recv.at[2 + t], at.d, at.partner
-            ).wait_recv()
-            add(cols.at[t])
-
-    base = 2 + at.chips
-    moves = []
-    for o in range(1, at.diag_size):
-        peer = (at.d + o) % at.diag_size
-        moves.append(
-            at.copy(
-                total.at[peer], slots.at[o - 1], send.at[2 + o], recv.at[base + o - 1], peer, at.c
+            lanes = slice(2 * self.states + z * width, 2 * self.states + (z + 1) * width)
+            self.total[z] = self.part[self.lo : self.hi, lanes] * keep
+
+        @pl.when(at.segment == at.q)
+        def _():
+            self.add(self.colsum)
+
+        @pl.when(at.mirror_folded)
+        def _():
+            self.mirror.wait_recv()
+            self.add(self.rows)
+
+        for t in range(at.chips):
+            @pl.when(jnp.logical_and(at.q != t, at.segment_of(t) == at.q))
+            def _():
+                at.copy(
+                    self.colsum, self.cols.at[t], self.send.at[2], self.recv.at[2 + t],
+                    at.d, at.partner,
+                ).wait_recv()
+                self.add(self.cols.at[t])
+
+        base = 2 + at.chips
+        self.moves = []
+        for o in range(1, at.diag_size):
+            peer = (at.d + o) % at.diag_size
+            self.moves.append(
+                at.copy(
+                    self.total.at[peer], self.slots.at[o - 1],
+                    self.send.at[2 + o], self.recv.at[base + o - 1], peer, at.c,
+                )
             )
-        )
-        moves[-1].start()
-    value = total[at.d]
-    for o, move in enumerate(moves):
-        move.wait_recv()
-        value = value + slots[o]
-    for move in moves:
-        move.wait_send()
-    pair.wait_send()
-
-    @pl.when(at.folded)
-    def _():
-        mirror.wait_send()
-
-    @pl.when(at.segment != at.q)
-    def _():
-        home.wait_send()
-
-    return value
+            self.moves[-1].start()
+
+    def result(self):
+        value = self.total[self.at.d]
+        for o, move in enumerate(self.moves):
+            move.wait_recv()
+            value = value + self.slots[o]
+        return value
+
+    def close(self):
+        for move in self.moves:
+            move.wait_send()
+        self.pair.wait_send()
+
+        @pl.when(self.at.folded)
+        def _():
+            self.mirror.wait_send()
+
+        @pl.when(self.at.segment != self.at.q)
+        def _():
+            self.home.wait_send()
 
 
 def along_diag(at, slots, send, recv):
@@ -345,45 +380,64 @@
         out_ref[:, i * states : (i + 1) * states] = vec[i]
 
 
-def search_kernel(
-    sizes, part, x_ref, slice_ref, search_ref, out_ref,
-    other, colsum, cols, rows, total, slots, by_diag, by_long, pieces, own, vec,
-    sum_send, sum_recv, z_send, z_recv, l_send, l_recv, s_send, s_recv, g_send, g_recv,
-):
+def search_kernel(sizes, part, x_ref, slice_ref, search_ref, out_ref, *scratch):
+    bufs_x, bufs_p = scratch[:6], scratch[6:12]
+    by_diag, by_long, pieces, own, vec = scratch[12:17]
+    send_x, recv_x, send_p, recv_p = scratch[17:21]
+    sums_sems, s_send, s_recv, g_send, g_recv = scratch[21:25], *scratch[25:29]
     at = Place(*sizes)
     at.enter()
-    image = sum_slices(at, part, other, colsum, cols, rows, total, slots, sum_send, sum_recv)
-    slice_ref[...] = image
     count, states = x_ref.shape
+    sum_x = PanelSum(at, part, 0, count, bufs_x, send_x, recv_x)
+    sum_p = PanelSum(at, part, count, 2 * count, bufs_p, send_p, recv_p)
+    sum_x.start()
+    sum_x.columns()
+    sum_p.start()
+    sum_x.totals()
+    sum_p.columns()
+    image = sum_x.result()
+    slice_ref[:count] = image
     width = image.shape[1]
-    image = image[:count]
     block = x_ref[:, pl.ds(pl.multiple_of(at.d * width, 128), width)].astype(jnp.float32)
     both = jnp.concatenate([block * image, block * block], 0)
     folded = both[:, :128]
     for i in range(1, width // 128):
         folded = folded + both[:, i * 128 : (i + 1) * 128]
-    sums = sum_all(at, folded, by_diag, by_long, (z_send, z_recv, l_send, l_recv))
+    sums = sum_all(at, folded, by_diag, by_long, sums_sems)
     sums = jnp.sum(sums, axis=1, keepdims=True)
     quotient = sums[:count] / sums[count:]
     pieces[at.d] = (image - quotient * block).astype(jnp.bfloat16)
-    finish(along_diag(at, pieces, s_send, s_recv))
+    moves = along_diag(at, pieces, s_send, s_recv)
+    sum_p.totals()
+    finish(moves)
     for z in range(at.diag_size):
         own[:, z * width : (z + 1) * width] = pieces[z]
     spread_panels(at, own, vec, g_send, g_recv)
     search_ref[...] = own[...]
     for i in range(3):
         out_ref[:, i * states : (i + 1) * states] = vec[i]
+    slice_ref[count:] = sum_p.result()
+    sum_x.close()
+    sum_p.close()
 
 
 def project_kernel(
     sizes, part, first_ref, x_ref, search_ref, p_ref, sums_ref, image_ref,
-    other, colsum, cols, rows, total, slots, by_diag, by_long, pieces, both,
-    sum_send, sum_recv, z_send, z_recv, l_send, l_recv, s_send, s_recv,
+    other, colsum, cols, rows, total, slots, by_diag, by_long, pieces, firsts, both,
+    sum_send, sum_recv, z_send, z_recv, l_send, l_recv, s_send, s_recv, f_send, f_recv,
 ):
     at = Place(*sizes)
     at.enter()
-    image = sum_slices(at, part, other, colsum, cols, rows, total, slots, sum_send, sum_recv)
-    count, width = image.shape
+    bufs = (other, colsum, cols, rows, total, slots)
+    count = x_ref.shape[0]
+    sum_w = PanelSum(at, part, 0, count, bufs, sum_send, sum_recv)
+    sum_w.start()
+    firsts[at.d] = first_ref[...]
+    first_moves = along_diag(at, firsts, f_send, f_recv)
+    sum_w.columns()
+    sum_w.totals()
+    image = sum_w.result()
+    width = image.shape[1]
     pieces[at.d] = image
     moves = along_diag(at, pieces, s_send, s_recv)
     lanes = pl.ds(pl.multiple_of(at.d * width, 128), width)
@@ -400,8 +454,13 @@
     )
     sums_ref[...] = sum_all(at, value, by_diag, by_long, (z_send, z_recv, l_send, l_recv))
     finish(moves)
+    finish(first_moves)
     for z in range(at.diag_size):
-        image_ref[:, z * width : (z + 1) * width] = pieces[z]
+        lanes = slice(z * width, (z + 1) * width)
+        image_ref[:count, lanes] = firsts[z, :count]
+        image_ref[count : 2 * count, lanes] = pieces[z]
+        image_ref[2 * count :, lanes] = firsts[z, count:]
+    sum_w.close()
 
 
 def sum_scratch(count, states, diag_size, long_size):
@@ -467,7 +526,7 @@
     first, search, vectors = remote_call(
         search_kernel, sizes, 2,
         [((2 * count, width), f32), ((count, states), bf16), ((count, 3 * states), bf16)],
-        sum_scratch(2 * count, states, *sizes)
+        sum_scratch(count, states, *sizes) * 2
         + [
             pltpu.VMEM((diag_size, 2 * count, 128), f32),
             pltpu.VMEM((long_size, 2 * count, 128), f32),
@@ -475,26 +534,25 @@
             pltpu.VMEM((count, states), bf16),
             pltpu.VMEM((3, count, states), bf16),
         ]
-        + sum_sems + all_sems + diag_sems + spread_sems,
+        + sum_sems * 2 + all_sems + diag_sems + spread_sems,
         part, block_x,
     )
-    first_whole = lax.all_gather(first, "diag", axis=1, tiled=True)
     part = apply_tiles(tile_block, rows, cols, meta, vectors)
-    sums, image_w = remote_call(
+    sums, himage = remote_call(
         project_kernel, sizes, 3,
-        [((3 * count, 128), f32), ((count, states), f32)],
+        [((3 * count, 128), f32), ((3 * count, states), f32)],
         sum_scratch(count, states, *sizes)
         + [
             pltpu.VMEM((diag_size, 3 * count, 128), f32),
             pltpu.VMEM((long_size, 3 * count, 128), f32),
             pltpu.VMEM((diag_size, count, width), f32),
+            pltpu.VMEM((diag_size, 2 * count, width), f32),
             pltpu.VMEM((128, width), f32),
         ]
-        + sum_sems + all_sems + diag_sems,
+        + sum_sems + all_sems + diag_sems * 2,
         part, first, block_x, search, block_p,
     )
     basis_in = jnp.concatenate([block_x, search, block_p], 0)
-    himage = jnp.concatenate([first_whole[:count], image_w, first_whole[count:]], 0)
     return tuple(ritz(sums, basis_in, himage))
 
 

time: 164 us -> 123 us (0.75)
  Pallas kernels: 144 us -> 118 us
  blocking collectives: 14.3 us -> 0 us
    all_gather x1 -> x0, blocking collectives: 14.3 us -> none  [local(): first_whole = lax.all_gather(first, 'diag', axis=1, tiled=True)]
    pallas_call x3, Pallas kernels: 104 us -> 90.2 us  [remote_call(): pl.pallas_call(functools.partial(kernel, sizes), in_specs=[vmem] * len(ar...]
    pallas_call x2, Pallas kernels: 34 us -> 21.7 us  [apply_tiles(): pl.pallas_call(tile_kernel, grid=(slots // STEP,), in_specs=[smem, smem,...]
where the time goes in v3:
time: 123 us
  Pallas kernels  118 us (96%)
  local copies, waits for them, and re-layouts  3.16 us (3%)
  between operations  1.4 us (1%)
    pallas_call x3, Pallas kernels, remote_call(): pl.pallas_call(functools.partial(kernel, sizes), in_specs=[vmem] * len(ar...  90.2 us
    pallas_call x2, Pallas kernels, apply_tiles(): pl.pallas_call(tile_kernel, grid=(slots // STEP,), in_specs=[smem, smem,...  21.7 us
    pallas_call x1, Pallas kernels, ritz(): pl.pallas_call(ritz_kernel, in_specs=[vmem] * 3, out_specs=[vmem] * 3, ou...  6.38 us
    unnamed x16, local copies, waits for them, and re-layouts  3.16 us

profile of v3, /device:TPU:0, one launch (start us, length us, event | category | flops | bytes accessed | tf_op | source)
XLA Modules:
  0.0 123.0 jit_solution(8692339643043345853)
XLA Ops:
  0.6 0.0 copy-start.7
  0.6 0.0 copy-start.5
  1.3 0.1 pad_add_fusion.meta_ref
  1.4 0.0 copy-start
  1.4 0.9 copy-done
  2.3 0.0 copy-start.2
  2.3 0.9 copy-done.2
  3.2 13.6 %shard_map.85.vec_ref = bf16[32,9216]{1,0:T(8,128)(2,1)S(1)} custom-call(bf16[16,3072]{1,0:T(8,128)(2,1)S(1)} %copy-done, bf16[16,3072]{1,0:T(8,128)(2,1)S(1)} %copy-done.2), custom_call_target="tpu_custom_call" | custom-call | tf_op jit(solution)/shard_map/pallas_call | solution.py:481
  16.7 0.0 copy-start.4
  16.8 0.7 copy-done.4
  17.4 0.0 copy-start.6
  17.4 0.7 copy-done.6
  18.1 0.0 copy-start.1
  18.1 0.0 copy-start.3
  18.1 11.0 %shard_map.86.part = f32[32,9216]{1,0:T(8,128)S(1)} custom-call(s32[512]{0:T(512)S(1)} %bitcast.7, s32[512]{0:T(512)S(1)} %bitcast.9, s32[3]{0:T(128)S(1)} %pad_add_fusion.meta_ref, bf16[32,9216]{1,0:T(8,128)(2,1)S(1)} %shard_map.85.vec_ref, bf16[512,128,128]{2,1,0:T(8,128)(2,1)} %bitcast.11), custom_call_target="tpu_custom_call" | custom-call | flops 1073741824 | bytes 16777216 | tf_op jit(solution)/shard_map/pallas_call | solution.py:75
  29.1 42.5 %shard_map.87 = (f32[32,768]{1,0:T(8,128)S(1)}, bf16[16,3072]{1,0:T(8,128)(2,1)S(1)}, bf16[16,9216]{1,0:T(8,128)(2,1)S(1)}) custom-call(f32[32,9216]{1,0:T(8,128)S(1)} %shard_map.86.part, bf16[16,3072]{1,0:T(8,128)(2,1)S(1)} %copy-done), custom_call_target="tpu_custom_call" | custom-call | tf_op jit(solution)/shard_map/pallas_call | solution.py:481
  71.6 0.0 copy-done.7
  71.6 0.0 copy-done.5
  71.6 10.7 %shard_map.88.part = f32[16,9216]{1,0:T(8,128)S(1)} custom-call(s32[512]{0:T(512)S(1)} %bitcast.8, s32[512]{0:T(512)S(1)} %bitcast.10, s32[3]{0:T(128)S(1)} %pad_add_fusion.meta_ref, bf16[16,9216]{1,0:T(8,128)(2,1)S(1)} %get-tuple-element.8.vec_ref, bf16[512,128,128]{2,1,0:T(8,128)(2,1)} %bitcast.12), custom_call_target="tpu_custom_call" | custom-call | flops 536870912 | bytes 16777216 | tf_op jit(solution)/shard_map/pallas_call | solution.py:75
  82.3 0.0 copy-done.1
  82.3 0.0 copy-done.3
  82.3 34.2 %shard_map.89 = (f32[48,128]{1,0:T(8,128)S(1)}, f32[48,3072]{1,0:T(8,128)S(1)}) custom-call(f32[16,9216]{1,0:T(8,128)S(1)} %shard_map.88.part, f32[32,768]{1,0:T(8,128)S(1)} %get-tuple-element.9.first_ref, bf16[16,3072]{1,0:T(8,128)(2,1)S(1)} %copy-done.1, bf16[16,3072]{1,0:T(8,128)(2,1)S(1)} %get-tuple-element.10.search_ref, bf16[16,3072]{1,0:T(8,128)(2,1)S(1)} %copy-done.3), custom_call_target="tpu_custom_call" | custom-call | tf_op jit(solution)/shard_map/pallas_call | solution.py:481
  116.6 6.4 %shard_map.90 = (f32[48,3072]{1,0:T(8,128)}, f32[48,3072]{1,0:T(8,128)}, f32[48,48]{1,0:T(8,128)}) custom-call(f32[48,128]{1,0:T(8,128)S(1)} %get-tuple-element.11.sums_ref, bf16[48,3072]{1,0:T(8,128)(2,1)S(1)} %pad_maximum_fusion.basis_ref, f32[48,3072]{1,0:T(8,128)S(1)} %get-tuple-element.12.image_ref), custom_call_target="tpu_custom_call" | custom-call | tf_op jit(solution)/shard_map/pallas_call | solution.py:129
  (1 shorter events, 0.0 us)
Async XLA Ops:
  0.6 70.9 %copy-start.7 = (s32[1,1,512]{2,1,0:T(1,128)S(1)}, s32[1,1,512]{2,1,0:T(1,128)}, u32[]{:S(2)}) copy-start(s32[1,1,512]{2,1,0:T(1,128)} %param.8) | copy-start | bytes 6148
  0.6 70.9 %copy-start.5 = (s32[1,1,512]{2,1,0:T(1,128)S(1)}, s32[1,1,512]{2,1,0:T(1,128)}, u32[]{:S(2)}) copy-start(s32[1,1,512]{2,1,0:T(1,128)} %param.7) | copy-start | bytes 6148
  1.4 0.9 copy-start
  2.3 0.9 copy-start.2
  16.7 0.7 copy-start.4
  17.4 0.7 copy-start.6
  18.1 64.2 %copy-start.1 = (bf16[16,3072]{1,0:T(8,128)(2,1)S(1)}, bf16[16,3072]{1,0:T(8,128)(2,1)}, u32[]{:S(2)}) copy-start(bf16[16,3072]{1,0:T(8,128)(2,1)} %x_ref.5) | copy-start | bytes 294916
  18.1 64.2 %copy-start.3 = (bf16[16,3072]{1,0:T(8,128)(2,1)S(1)}, bf16[16,3072]{1,0:T(8,128)(2,1)}, u32[]{:S(2)}) copy-start(bf16[16,3072]{1,0:T(8,128)(2,1)} %p_ref.3) | copy-start | bytes 294916

commit v4 on v3

--- a/solution.py
+++ b/solution.py
@@ -225,99 +225,107 @@
         self.at, self.part, self.lo, self.hi = at, part, lo, hi
         self.other, self.colsum, self.cols, self.rows, self.total, self.slots = bufs
         self.send, self.recv = send, recv
-        self.states, self.width = self.other.shape[1], self.total.shape[2]
-        states = self.states
-        self.mine = pl.ds(pl.multiple_of(at.k * states, 128), states)
-        theirs = pl.ds(pl.multiple_of((1 - at.k) * states, 128), states)
-        self.pair = at.copy(
-            part.at[lo:hi, theirs], self.other, send.at[0], recv.at[0], at.d, at.partner
-        )
-        self.mirror = at.copy(
-            part.at[lo:hi, pl.ds(2 * states, states)],
-            self.rows, send.at[1], recv.at[1], at.d, at.mirror,
-        )
-        self.home = at.copy(
-            self.colsum, self.cols.at[at.q], send.at[2], recv.at[2 + at.q],
-            at.d, 2 * at.segment + at.k,
+        size = at.diag_size
+        self.width = self.total.shape[2]
+        self.states = self.width * size
+        self.order = [(o, (at.d + o) % size) for o in [*range(1, size), 0]]
+
+    def lanes(self, panel, z):
+        start = pl.multiple_of(panel * self.states + z * self.width, 128)
+        return pl.ds(start, self.width)
+
+    def pair(self, o, z):
+        at = self.at
+        return at.copy(
+            self.part.at[self.lo : self.hi, self.lanes(1 - at.k, z)], self.other.at[z],
+            self.send.at[o], self.recv.at[o], at.d, at.partner,
+        )
+
+    def mirror(self, o, z):
+        at, size = self.at, self.at.diag_size
+        return at.copy(
+            self.part.at[self.lo : self.hi, self.lanes(2, z)], self.rows.at[z],
+            self.send.at[size + o], self.recv.at[size + o], at.d, at.mirror,
+        )
+
+    def home(self, o, z, slot, chip):
+        at, size = self.at, self.at.diag_size
+        return at.copy(
+            self.colsum.at[z], self.cols.at[slot, z],
+            self.send.at[2 * size + o], self.recv.at[(2 + slot) * size + o],
+            at.d, chip,
+        )
+
+    def move(self, o, z):
+        at, size = self.at, self.at.diag_size
+        return at.copy(
+            self.total.at[z], self.slots.at[o - 1],
+            self.send.at[3 * size + o - 1], self.recv.at[(2 + at.chips) * size + o - 1], z, at.c,
         )
 
     def start(self):
-        self.pair.start()
-
-        @pl.when(self.at.folded)
-        def _():
-            self.mirror.start()
+        for o, z in self.order:
+            self.pair(o, z).start()
+
+            @pl.when(self.at.folded)
+            def _():
+                self.mirror(o, z).start()
 
     def columns(self):
         at = self.at
-        self.pair.wait_recv()
-        self.colsum[...] = self.part[self.lo : self.hi, self.mine] + self.other[...]
-
-        @pl.when(at.segment != at.q)
-        def _():
-            self.home.start()
-
-    def add(self, panel):
-        width = self.width
-        for z in range(self.at.diag_size):
-            self.total[z] += panel[:, z * width : (z + 1) * width]
+        for o, z in self.order:
+            self.pair(o, z).wait_recv()
+            self.colsum[z] = self.part[self.lo : self.hi, self.lanes(at.k, z)] + self.other[z]
+
+            @pl.when(at.segment != at.q)
+            def _():
+                self.home(o, z, at.q, 2 * at.segment + at.k).start()
 
     def totals(self):
-        at, width = self.at, self.width
+        at = self.at
         keep = jnp.where(at.folded, 0.0, 1.0).astype(jnp.float32)
-        for z in range(at.diag_size):
-            lanes = slice(2 * self.states + z * width, 2 * self.states + (z + 1) * width)
-            self.total[z] = self.part[self.lo : self.hi, lanes] * keep
-
-        @pl.when(at.segment == at.q)
-        def _():
-            self.add(self.colsum)
-
-        @pl.when(at.mirror_folded)
-        def _():
-            self.mirror.wait_recv()
-            self.add(self.rows)
-
-        for t in range(at.chips):
-            @pl.when(jnp.logical_and(at.q != t, at.segment_of(t) == at.q))
+        for o, z in self.order:
+            self.total[z] = self.part[self.lo : self.hi, self.lanes(2, z)] * keep
+
+            @pl.when(at.segment == at.q)
             def _():
-                at.copy(
-                    self.colsum, self.cols.at[t], self.send.at[2], self.recv.at[2 + t],
-                    at.d, at.partner,
-                ).wait_recv()
-                self.add(self.cols.at[t])
-
-        base = 2 + at.chips
-        self.moves = []
-        for o in range(1, at.diag_size):
-            peer = (at.d + o) % at.diag_size
-            self.moves.append(
-                at.copy(
-                    self.total.at[peer], self.slots.at[o - 1],
-                    self.send.at[2 + o], self.recv.at[base + o - 1], peer, at.c,
-                )
-            )
-            self.moves[-1].start()
+                self.total[z] += self.colsum[z]
+
+            @pl.when(at.mirror_folded)
+            def _():
+                self.mirror(o, z).wait_recv()
+                self.total[z] += self.rows[z]
+
+            for t in range(at.chips):
+                @pl.when(jnp.logical_and(at.q != t, at.segment_of(t) == at.q))
+                def _():
+                    self.home(o, z, t, at.partner).wait_recv()
+                    self.total[z] += self.cols[t, z]
+
+            if o:
+                self.move(o, z).start()
 
     def result(self):
         value = self.total[self.at.d]
-        for o, move in enumerate(self.moves):
-            move.wait_recv()
-            value = value + self.slots[o]
+        for o, z in self.order[:-1]:
+            self.move(o, z).wait_recv()
+            value = value + self.slots[o - 1]
         return value
 
     def close(self):
-        for move in self.moves:
-            move.wait_send()
-        self.pair.wait_send()
-
-        @pl.when(self.at.folded)
-        def _():
-            self.mirror.wait_send()
-
-        @pl.when(self.at.segment != self.at.q)
-        def _():
-            self.home.wait_send()
+        at = self.at
+        for o, z in self.order:
+            if o:
+                self.move(o, z).wait_send()
+            self.pair(o, z).wait_send()
+
+            @pl.when(at.folded)
+            def _():
+                self.mirror(o, z).wait_send()
+
+            @pl.when(at.segment != at.q)
+            def _():
+                self.home(o, z, at.q, 2 * at.segment + at.k).wait_send()
 
 
 def along_diag(at, slots, send, recv):
@@ -465,13 +473,14 @@
 
 def sum_scratch(count, states, diag_size, long_size):
     width = states // diag_size
+    panel = (diag_size, count, width)
     f32 = jnp.float32
     return [
-        pltpu.VMEM((count, states), f32),
-        pltpu.VMEM((count, states), f32),
-        pltpu.VMEM((long_size // 2, count, states), f32),
-        pltpu.VMEM((count, states), f32),
-        pltpu.VMEM((diag_size, count, width), f32),
+        pltpu.VMEM(panel, f32),
+        pltpu.VMEM(panel, f32),
+        pltpu.VMEM((long_size // 2, *panel), f32),
+        pltpu.VMEM(panel, f32),
+        pltpu.VMEM(panel, f32),
         pltpu.VMEM((diag_size - 1, count, width), f32),
     ]
 
@@ -512,7 +521,7 @@
     chips = long_size // 2
     f32, bf16, dma = jnp.float32, jnp.bfloat16, pltpu.SemaphoreType.DMA
     spread_sems = [dma((chips + 2,)), dma((3,))]
-    sum_sems = [dma((diag_size + 2,)), dma((1 + chips + diag_size,))]
+    sum_sems = [dma((4 * diag_size - 1,)), dma(((3 + chips) * diag_size - 1,))]
     all_sems = [dma((n - 1,)) for n in (diag_size, diag_size, long_size, long_size)]
     diag_sems = [dma((diag_size - 1,))] * 2
 

time: 123 us -> 120 us (0.976)
  Pallas kernels: 118 us -> 116 us
    pallas_call x3, Pallas kernels: 90.2 us -> 87.5 us  [remote_call(): pl.pallas_call(functools.partial(kernel, sizes), in_specs=[vmem] * len(ar...]
where the time goes in v4:
time: 120 us
  Pallas kernels  116 us (97%)
  local copies, waits for them, and re-layouts  3.16 us (3%)
  between operations  1.4 us (1%)
    pallas_call x3, Pallas kernels, remote_call(): pl.pallas_call(functools.partial(kernel, sizes), in_specs=[vmem] * len(ar...  87.5 us
    pallas_call x2, Pallas kernels, apply_tiles(): pl.pallas_call(tile_kernel, grid=(slots // STEP,), in_specs=[smem, smem,...  21.7 us
    pallas_call x1, Pallas kernels, ritz(): pl.pallas_call(ritz_kernel, in_specs=[vmem] * 3, out_specs=[vmem] * 3, ou...  6.38 us
    unnamed x16, local copies, waits for them, and re-layouts  3.16 us

profile of v4, /device:TPU:0, one launch (start us, length us, event | category | flops | bytes accessed | tf_op | source)
XLA Modules:
  0.0 120.2 jit_solution(18231018389385132031)
XLA Ops:
  0.6 0.0 copy-start.7
  0.6 0.0 copy-start.5
  1.3 0.1 pad_add_fusion.meta_ref
  1.4 0.0 copy-start
  1.4 0.9 copy-done
  2.3 0.0 copy-start.2
  2.3 0.9 copy-done.2
  3.2 13.6 %shard_map.85.vec_ref = bf16[32,9216]{1,0:T(8,128)(2,1)S(1)} custom-call(bf16[16,3072]{1,0:T(8,128)(2,1)S(1)} %copy-done, bf16[16,3072]{1,0:T(8,128)(2,1)S(1)} %copy-done.2), custom_call_target="tpu_custom_call" | custom-call | tf_op jit(solution)/shard_map/pallas_call | solution.py:490
  16.7 0.0 copy-start.4
  16.8 0.7 copy-done.4
  17.4 0.0 copy-start.6
  17.4 0.7 copy-done.6
  18.1 0.0 copy-start.1
  18.1 0.0 copy-start.3
  18.1 11.0 %shard_map.86.part = f32[32,9216]{1,0:T(8,128)S(1)} custom-call(s32[512]{0:T(512)S(1)} %bitcast.7, s32[512]{0:T(512)S(1)} %bitcast.9, s32[3]{0:T(128)S(1)} %pad_add_fusion.meta_ref, bf16[32,9216]{1,0:T(8,128)(2,1)S(1)} %shard_map.85.vec_ref, bf16[512,128,128]{2,1,0:T(8,128)(2,1)} %bitcast.11), custom_call_target="tpu_custom_call" | custom-call | flops 1073741824 | bytes 16777216 | tf_op jit(solution)/shard_map/pallas_call | solution.py:75
  29.1 40.5 %shard_map.87 = (f32[32,768]{1,0:T(8,128)S(1)}, bf16[16,3072]{1,0:T(8,128)(2,1)S(1)}, bf16[16,9216]{1,0:T(8,128)(2,1)S(1)}) custom-call(f32[32,9216]{1,0:T(8,128)S(1)} %shard_map.86.part, bf16[16,3072]{1,0:T(8,128)(2,1)S(1)} %copy-done), custom_call_target="tpu_custom_call" | custom-call | tf_op jit(solution)/shard_map/pallas_call | solution.py:490
  69.6 0.0 copy-done.7
  69.7 0.0 copy-done.5
  69.7 10.7 %shard_map.88.part = f32[16,9216]{1,0:T(8,128)S(1)} custom-call(s32[512]{0:T(512)S(1)} %bitcast.8, s32[512]{0:T(512)S(1)} %bitcast.10, s32[3]{0:T(128)S(1)} %pad_add_fusion.meta_ref, bf16[16,9216]{1,0:T(8,128)(2,1)S(1)} %get-tuple-element.8.vec_ref, bf16[512,128,128]{2,1,0:T(8,128)(2,1)} %bitcast.12), custom_call_target="tpu_custom_call" | custom-call | flops 536870912 | bytes 16777216 | tf_op jit(solution)/shard_map/pallas_call | solution.py:75
  80.4 0.0 copy-done.1
  80.4 0.0 copy-done.3
  80.4 33.4 %shard_map.89 = (f32[48,128]{1,0:T(8,128)S(1)}, f32[48,3072]{1,0:T(8,128)S(1)}) custom-call(f32[16,9216]{1,0:T(8,128)S(1)} %shard_map.88.part, f32[32,768]{1,0:T(8,128)S(1)} %get-tuple-element.9.first_ref, bf16[16,3072]{1,0:T(8,128)(2,1)S(1)} %copy-done.1, bf16[16,3072]{1,0:T(8,128)(2,1)S(1)} %get-tuple-element.10.search_ref, bf16[16,3072]{1,0:T(8,128)(2,1)S(1)} %copy-done.3), custom_call_target="tpu_custom_call" | custom-call | tf_op jit(solution)/shard_map/pallas_call | solution.py:490
  113.8 6.4 %shard_map.90 = (f32[48,3072]{1,0:T(8,128)}, f32[48,3072]{1,0:T(8,128)}, f32[48,48]{1,0:T(8,128)}) custom-call(f32[48,128]{1,0:T(8,128)S(1)} %get-tuple-element.11.sums_ref, bf16[48,3072]{1,0:T(8,128)(2,1)S(1)} %pad_maximum_fusion.basis_ref, f32[48,3072]{1,0:T(8,128)S(1)} %get-tuple-element.12.image_ref), custom_call_target="tpu_custom_call" | custom-call | tf_op jit(solution)/shard_map/pallas_call | solution.py:129
  (1 shorter events, 0.0 us)
Async XLA Ops:
  0.6 69.0 %copy-start.7 = (s32[1,1,512]{2,1,0:T(1,128)S(1)}, s32[1,1,512]{2,1,0:T(1,128)}, u32[]{:S(2)}) copy-start(s32[1,1,512]{2,1,0:T(1,128)} %param.8) | copy-start | bytes 6148
  0.6 69.0 %copy-start.5 = (s32[1,1,512]{2,1,0:T(1,128)S(1)}, s32[1,1,512]{2,1,0:T(1,128)}, u32[]{:S(2)}) copy-start(s32[1,1,512]{2,1,0:T(1,128)} %param.7) | copy-start | bytes 6148
  1.4 0.9 copy-start
  2.3 0.9 copy-start.2
  16.7 0.7 copy-start.4
  17.4 0.7 copy-start.6
  18.1 62.3 %copy-start.1 = (bf16[16,3072]{1,0:T(8,128)(2,1)S(1)}, bf16[16,3072]{1,0:T(8,128)(2,1)}, u32[]{:S(2)}) copy-start(bf16[16,3072]{1,0:T(8,128)(2,1)} %x_ref.5) | copy-start | bytes 294916
  18.1 62.3 %copy-start.3 = (bf16[16,3072]{1,0:T(8,128)(2,1)S(1)}, bf16[16,3072]{1,0:T(8,128)(2,1)}, u32[]{:S(2)}) copy-start(bf16[16,3072]{1,0:T(8,128)(2,1)} %p_ref.3) | copy-start | bytes 294916

commit v5 on v4

--- a/solution.py
+++ b/solution.py
@@ -9,7 +9,7 @@
 
 HIGHEST = lax.Precision.HIGHEST
 STEP = 64
-UNROLL = 32
+UNROLL = 64
 
 
 def tile_kernel(rows_ref, cols_ref, meta_ref, vec_ref, tile_ref, out_ref):

time: 120 us -> 120 us (level)
  no operation moved by 1% of the time
where the time goes in v5:
time: 120 us
  Pallas kernels  115 us (96%)
  local copies, waits for them, and re-layouts  3.16 us (3%)
  between operations  1.4 us (1%)
    pallas_call x3, Pallas kernels, remote_call(): pl.pallas_call(functools.partial(kernel, sizes), in_specs=[vmem] * len(ar...  88.1 us
    pallas_call x2, Pallas kernels, apply_tiles(): pl.pallas_call(tile_kernel, grid=(slots // STEP,), in_specs=[smem, smem,...  20.9 us
    pallas_call x1, Pallas kernels, ritz(): pl.pallas_call(ritz_kernel, in_specs=[vmem] * 3, out_specs=[vmem] * 3, ou...  6.38 us
    unnamed x16, local copies, waits for them, and re-layouts  3.16 us

profile of v5, /device:TPU:0, one launch (start us, length us, event | category | flops | bytes accessed | tf_op | source)
XLA Modules:
  0.0 120.1 jit_solution(10955232282325991714)
XLA Ops:
  0.6 0.0 copy-start.7
  0.6 0.0 copy-start.5
  1.3 0.1 pad_add_fusion.meta_ref
  1.4 0.0 copy-start
  1.4 0.9 copy-done
  2.3 0.0 copy-start.2
  2.3 0.9 copy-done.2
  3.2 13.6 %shard_map.85.vec_ref = bf16[32,9216]{1,0:T(8,128)(2,1)S(1)} custom-call(bf16[16,3072]{1,0:T(8,128)(2,1)S(1)} %copy-done, bf16[16,3072]{1,0:T(8,128)(2,1)S(1)} %copy-done.2), custom_call_target="tpu_custom_call" | custom-call | tf_op jit(solution)/shard_map/pallas_call | solution.py:490
  16.7 0.0 copy-start.4
  16.8 0.7 copy-done.4
  17.4 0.0 copy-start.6
  17.4 0.7 copy-done.6
  18.1 0.0 copy-start.1
  18.1 0.0 copy-start.3
  18.1 10.6 %shard_map.86.part = f32[32,9216]{1,0:T(8,128)S(1)} custom-call(s32[512]{0:T(512)S(1)} %bitcast.7, s32[512]{0:T(512)S(1)} %bitcast.9, s32[3]{0:T(128)S(1)} %pad_add_fusion.meta_ref, bf16[32,9216]{1,0:T(8,128)(2,1)S(1)} %shard_map.85.vec_ref, bf16[512,128,128]{2,1,0:T(8,128)(2,1)} %bitcast.11), custom_call_target="tpu_custom_call" | custom-call | flops 1073741824 | bytes 16777216 | tf_op jit(solution)/shard_map/pallas_call | solution.py:75
  28.7 40.0 %shard_map.87 = (f32[32,768]{1,0:T(8,128)S(1)}, bf16[16,3072]{1,0:T(8,128)(2,1)S(1)}, bf16[16,9216]{1,0:T(8,128)(2,1)S(1)}) custom-call(f32[32,9216]{1,0:T(8,128)S(1)} %shard_map.86.part, bf16[16,3072]{1,0:T(8,128)(2,1)S(1)} %copy-done), custom_call_target="tpu_custom_call" | custom-call | tf_op jit(solution)/shard_map/pallas_call | solution.py:490
  68.7 0.0 copy-done.7
  68.7 0.0 copy-done.5
  68.7 10.3 %shard_map.88.part = f32[16,9216]{1,0:T(8,128)S(1)} custom-call(s32[512]{0:T(512)S(1)} %bitcast.8, s32[512]{0:T(512)S(1)} %bitcast.10, s32[3]{0:T(128)S(1)} %pad_add_fusion.meta_ref, bf16[16,9216]{1,0:T(8,128)(2,1)S(1)} %get-tuple-element.8.vec_ref, bf16[512,128,128]{2,1,0:T(8,128)(2,1)} %bitcast.12), custom_call_target="tpu_custom_call" | custom-call | flops 536870912 | bytes 16777216 | tf_op jit(solution)/shard_map/pallas_call | solution.py:75
  79.1 0.0 copy-done.1
  79.1 0.0 copy-done.3
  79.1 34.6 %shard_map.89 = (f32[48,128]{1,0:T(8,128)S(1)}, f32[48,3072]{1,0:T(8,128)S(1)}) custom-call(f32[16,9216]{1,0:T(8,128)S(1)} %shard_map.88.part, f32[32,768]{1,0:T(8,128)S(1)} %get-tuple-element.9.first_ref, bf16[16,3072]{1,0:T(8,128)(2,1)S(1)} %copy-done.1, bf16[16,3072]{1,0:T(8,128)(2,1)S(1)} %get-tuple-element.10.search_ref, bf16[16,3072]{1,0:T(8,128)(2,1)S(1)} %copy-done.3), custom_call_target="tpu_custom_call" | custom-call | tf_op jit(solution)/shard_map/pallas_call | solution.py:490
  113.7 6.4 %shard_map.90 = (f32[48,3072]{1,0:T(8,128)}, f32[48,3072]{1,0:T(8,128)}, f32[48,48]{1,0:T(8,128)}) custom-call(f32[48,128]{1,0:T(8,128)S(1)} %get-tuple-element.11.sums_ref, bf16[48,3072]{1,0:T(8,128)(2,1)S(1)} %pad_maximum_fusion.basis_ref, f32[48,3072]{1,0:T(8,128)S(1)} %get-tuple-element.12.image_ref), custom_call_target="tpu_custom_call" | custom-call | tf_op jit(solution)/shard_map/pallas_call | solution.py:129
  (1 shorter events, 0.0 us)
Async XLA Ops:
  0.6 68.1 %copy-start.7 = (s32[1,1,512]{2,1,0:T(1,128)S(1)}, s32[1,1,512]{2,1,0:T(1,128)}, u32[]{:S(2)}) copy-start(s32[1,1,512]{2,1,0:T(1,128)} %param.8) | copy-start | bytes 6148
  0.6 68.1 %copy-start.5 = (s32[1,1,512]{2,1,0:T(1,128)S(1)}, s32[1,1,512]{2,1,0:T(1,128)}, u32[]{:S(2)}) copy-start(s32[1,1,512]{2,1,0:T(1,128)} %param.7) | copy-start | bytes 6148
  1.4 0.9 copy-start
  2.3 0.9 copy-start.2
  16.7 0.7 copy-start.4
  17.4 0.7 copy-start.6
  18.1 60.9 %copy-start.1 = (bf16[16,3072]{1,0:T(8,128)(2,1)S(1)}, bf16[16,3072]{1,0:T(8,128)(2,1)}, u32[]{:S(2)}) copy-start(bf16[16,3072]{1,0:T(8,128)(2,1)} %x_ref.5) | copy-start | bytes 294916
  18.1 61.0 %copy-start.3 = (bf16[16,3072]{1,0:T(8,128)(2,1)S(1)}, bf16[16,3072]{1,0:T(8,128)(2,1)}, u32[]{:S(2)}) copy-start(bf16[16,3072]{1,0:T(8,128)(2,1)} %p_ref.3) | copy-start | bytes 294916
